TPU v7x, 256 devices: a whole 4x4x8 slice. The times are simulated.
256 devices in a mesh: gx: 16 (over x_lo, z), gy: 16 (over y, x_hi, core).
Axes of the slice: x: 4 (x_hi: 2, x_lo: 2; x = x_hi * 2 + x_lo), y: 4, z: 8, core: 2. Of those that a mesh axis runs over, the one named last changes fastest.
Arguments:
- features: bfloat16 [128, 128, 8, 128], P('gx', 'gy'), may hold values from -6 to 6
- weight_fine: bfloat16 [27, 128, 128], replicated, may hold values from -0.109375 to 0.109375
- weight_down: bfloat16 [27, 128, 256], replicated, may hold values from -0.109375 to 0.109375
- weight_mid: bfloat16 [27, 256, 256], replicated, may hold values from -0.078125 to 0.078125
- cotangent: bfloat16 [64, 64, 4, 256], P('gx', 'gy'), may hold values from -24 to 24
Outputs:
- grad_features: bfloat16 [128, 128, 8, 128], P('gx', 'gy')
- grad_fine: float32 [128, 27, 128], P('gx', None, 'gy')
- grad_down: float32 [128, 27, 256], P('gx', None, 'gy')
- grad_mid: float32 [256, 27, 256], P('gx', None, 'gy')
All inputs are finite; a program needn't handle non-finite values.
Results may differ from a plain program's by a relative error of at most 0.014.
Values may be sent and summed in bfloat16 or wider, within the bound.
A program may use at most 128 MiB of HBM per device.

v0:
```python
import math

import jax
import jax.numpy as jnp
from jax import lax
from jax.sharding import PartitionSpec as P

OFFSETS = [(i, j, k) for i in range(3) for j in range(3) for k in range(3)]


def extended(cells, sides, width):
    for axis, dim in sides:
        count = lax.axis_size(axis)
        ends = count - 1
        head = lax.slice_in_dim(cells, 0, width, axis=dim)
        tail = lax.slice_in_dim(cells, cells.shape[dim] - width, cells.shape[dim], axis=dim)
        cells = jnp.concatenate(
            [
                lax.ppermute(tail, axis, [(i, (i + 1) % count) for i in range(ends)]),
                cells,
                lax.ppermute(head, axis, [((i + 1) % count, i) for i in range(ends)]),
            ],
            axis=dim,
        )
    return cells


def deepen(field):
    return jnp.pad(field, ((0, 0), (0, 0), (1, 1), (0, 0)))


def convolve(ext, weight, size_x, size_y, size_z):
    chans = ext.shape[3]
    total = jnp.zeros((size_x * size_y * size_z, weight.shape[2]), jnp.float32)
    for index, (i, j, k) in enumerate(OFFSETS):
        piece = ext[i : i + size_x, j : j + size_y, k : k + size_z].reshape(
            size_x * size_y * size_z, chans
        )
        total = total + jnp.dot(piece, weight[index], preferred_element_type=jnp.float32)
    return total.reshape(size_x, size_y, size_z, weight.shape[2])


def adjoint(ext, weight, size_x, size_y, size_z):
    chans = ext.shape[3]
    total = jnp.zeros((size_x * size_y * size_z, weight.shape[1]), jnp.float32)
    for index, (i, j, k) in enumerate(OFFSETS):
        piece = ext[2 - i : 2 - i + size_x, 2 - j : 2 - j + size_y, 2 - k : 2 - k + size_z].reshape(
            size_x * size_y * size_z, chans
        )
        total = total + lax.dot_general(
            piece, weight[index], (((1,), (1,)), ((), ())), preferred_element_type=jnp.float32
        )
    return total.reshape(size_x, size_y, size_z, weight.shape[1])


def weight_grad(ext, grad):
    size_x, size_y, size_z, out_chans = grad.shape
    flat_grad = grad.reshape(size_x * size_y * size_z, out_chans)
    terms = []
    for i, j, k in OFFSETS:
        piece = ext[i : i + size_x, j : j + size_y, k : k + size_z].reshape(
            size_x * size_y * size_z, ext.shape[3]
        )
        terms.append(
            lax.dot_general(
                piece, flat_grad, (((0,), (0,)), ((), ())), preferred_element_type=jnp.float32
            )
        )
    return jnp.stack(terms, axis=1)


def slope(pre):
    sig = jax.nn.sigmoid(pre)
    return sig * (1.0 + pre * (1.0 - sig))


def spread(term):
    partial_sum = lax.psum_scatter(term, "gx", scatter_dimension=0, tiled=True)
    return lax.psum_scatter(partial_sum, "gy", scatter_dimension=2, tiled=True)


def per_device(features, weight_fine, weight_down, weight_mid, cotangent):
    fine_x, fine_y, fine_z, chans_fine = features.shape
    coarse_x, coarse_y, coarse_z = (fine_x // 2, fine_y // 2, fine_z // 2)
    count_x = lax.axis_size("gx")
    count_y = lax.axis_size("gy")
    feat_ext = deepen(extended(features, (("gx", 0), ("gy", 1)), 1))
    pre_fine = convolve(feat_ext, weight_fine, fine_x, fine_y, fine_z)
    act_fine = jax.nn.silu(pre_fine)
    pooled = (
        act_fine.reshape(coarse_x, 2, coarse_y, 2, coarse_z, 2, chans_fine)
        .mean(axis=(1, 3, 5))
        .astype(jnp.bfloat16)
    )
    pooled_ext = deepen(extended(pooled, (("gx", 0), ("gy", 1)), 1))
    pre_coarse = convolve(pooled_ext, weight_down, coarse_x, coarse_y, coarse_z)
    act_coarse = jax.nn.silu(pre_coarse).astype(jnp.bfloat16)
    act_ext = deepen(extended(act_coarse, (("gx", 0), ("gy", 1)), 1))
    cot_ext = deepen(extended(cotangent, (("gx", 0), ("gy", 1)), 1))
    delta_act = adjoint(cot_ext, weight_mid, coarse_x, coarse_y, coarse_z)
    delta_coarse = (delta_act * slope(pre_coarse)).astype(jnp.bfloat16)
    delta_ext = deepen(extended(delta_coarse, (("gx", 0), ("gy", 1)), 1))
    delta_pool = adjoint(delta_ext, weight_down, coarse_x, coarse_y, coarse_z)
    spread_up = jnp.broadcast_to(
        delta_pool[:, None, :, None, :, None, :],
        (coarse_x, 2, coarse_y, 2, coarse_z, 2, chans_fine),
    ).reshape(fine_x, fine_y, fine_z, chans_fine)
    delta_fine = (spread_up * 0.125 * slope(pre_fine)).astype(jnp.bfloat16)
    fine_ext = deepen(extended(delta_fine, (("gx", 0), ("gy", 1)), 1))
    grad_features = adjoint(fine_ext, weight_fine, fine_x, fine_y, fine_z).astype(jnp.bfloat16)
    fine_scale = math.sqrt(fine_x * count_x * fine_y * count_y * fine_z)
    coarse_scale = math.sqrt(coarse_x * count_x * coarse_y * count_y * coarse_z)
    grad_mid = spread(weight_grad(act_ext, cotangent)) / coarse_scale
    grad_down = spread(weight_grad(pooled_ext, delta_coarse)) / coarse_scale
    grad_fine = spread(weight_grad(feat_ext, delta_fine)) / fine_scale
    return (grad_features, grad_fine, grad_down, grad_mid)


def solution(mesh):
    in_specs = (P("gx", "gy", None, None), P(), P(), P(), P("gx", "gy", None, None))
    out_specs = (
        P("gx", "gy", None, None),
        P("gx", None, "gy"),
        P("gx", None, "gy"),
        P("gx", None, "gy"),
    )
    return jax.shard_map(
        per_device, mesh=mesh, in_specs=in_specs, out_specs=out_specs, check_vma=False
    )
```

profile of v0, /device:TPU:1, one launch (start us, length us, event | category | flops | bytes accessed | tf_op | source)
XLA Modules:
  0.0 753.0 jit_solution(1701588073277609211)
XLA Ops:
  10.0 5.0 collective-permute-start
  17.6 4.8 collective-permute-start.4
  29.4 5.9 collective-permute-start.2
  43.0 5.1 collective-permute-start.6
  119.7 3.0 collective-permute-start.8
  128.4 6.3 collective-permute-start.10
  136.7 4.5 collective-permute-done.11
  149.8 4.8 collective-permute-start.12
  168.4 2.9 collective-permute-start.15
  280.3 4.3 collective-permute-start.20
  285.9 3.7 collective-permute-done.21
  289.6 4.7 collective-permute-start.22
  296.3 4.7 collective-permute-done.23
  326.9 3.4 collective-permute-start.16
  331.6 4.5 collective-permute-done.17
  336.2 3.6 collective-permute-start.18
  342.6 4.5 collective-permute-done.19
  355.5 58.0 %reduce-scatter.11.cloned.1.call-done = f32[8,27,256]{2,0,1:T(8,128)} async-done(((f32[128,27,256]{2,0,1:T(8,128)}), f32[8,27,256]{2,0,1:T(8,128)}) %reduce-scatter.11.cloned.1.call-update) | async-done | bytes 221200 | tf_op jit(solution)/shard_map/reduce_scatter | solution.py:78
  413.4 2.4 copy.15
  416.3 91.7 %reduce-scatter.15.cloned.1.call-done = f32[16,27,256]{2,0,1:T(8,128)} async-done(((f32[256,27,256]{2,0,1:T(8,128)}), f32[16,27,256]{2,0,1:T(8,128)}) %reduce-scatter.15.cloned.1.call-update) | async-done | bytes 442384 | tf_op jit(solution)/shard_map/reduce_scatter | solution.py:78
  508.0 3.5 copy.16
  512.4 72.3 %reduce-scatter.9.cloned.1.call-done = f32[8,27,8]{1,0,2:T(8,128)} async-done(((f32[8,27,128]{1,0,2:T(8,128)}), f32[8,27,8]{1,0,2:T(8,128)}) %reduce-scatter.9.cloned.1.call-update) | async-done | bytes 6928 | tf_op jit(solution)/shard_map/reduce_scatter | solution.py:79
  586.0 76.7 %reduce-scatter.13.cloned.1.call-done = f32[8,27,16]{1,0,2:T(8,128)} async-done(((f32[8,27,256]{1,0,2:T(8,128)}), f32[8,27,16]{1,0,2:T(8,128)}) %reduce-scatter.13.cloned.1.call-update) | async-done | bytes 13840 | tf_op jit(solution)/shard_map/reduce_scatter | solution.py:79
  664.3 80.3 %reduce-scatter.17.cloned.1.call-done = f32[16,27,16]{1,0,2:T(8,128)} async-done(((f32[16,27,256]{1,0,2:T(8,128)}), f32[16,27,16]{1,0,2:T(8,128)}) %reduce-scatter.17.cloned.1.call-update) | async-done | bytes 27664 | tf_op jit(solution)/shard_map/reduce_scatter | solution.py:79
  (475 shorter events, 277.0 us)
Async XLA Ops:
  7.2 346.1 %reduce-scatter.7.cloned.1.call-start = ((), (), s32[]{:S(2)}) async-start(), calls=%async_computation.6 | async-start | bytes 1880064 | tf_op jit(solution)/shard_map/reduce_scatter | solution.py:78
  8.7 15.1 %collective-permute-start.1 = (bf16[1,4,4,256]{3,2,1,0:T(4,128)(2,1)}, bf16[1,4,4,256]{3,2,1,0:T(4,128)(2,1)S(1)}, u32[]{:S(2)}, u32[]{:S(2)}) collective-permute-start(bf16[1,4,4,256]{3,2,1,0:T(4,128)(2,1)} %get-tuple-element.166), channel_id=1, source_target_pairs={{16,0},{32,16},{48,32},{64,48},{80,64},{96,80},{112,96},{128,112},... | collective-permute-start | bytes 24584 | tf_op jit(solution)/shard_map/ppermute | solution.py:21
  10.0 13.8 %collective-permute-start = (bf16[1,4,4,256]{3,2,1,0:T(4,128)(2,1)}, bf16[1,4,4,256]{3,2,1,0:T(4,128)(2,1)S(1)}, u32[]{:S(2)}, u32[]{:S(2)}) collective-permute-start(bf16[1,4,4,256]{3,2,1,0:T(4,128)(2,1)} %get-tuple-element.167), channel_id=1, source_target_pairs={{0,16},{16,32},{32,48},{48,64},{64,80},{80,96},{96,112},{112,128},... | collective-permute-start | bytes 24584 | tf_op jit(solution)/shard_map/ppermute | solution.py:19
  16.3 23.9 %collective-permute-start.5 = (bf16[1,8,8,128]{3,2,1,0:T(8,128)(2,1)}, bf16[1,8,8,128]{3,2,1,0:T(8,128)(2,1)}, u32[]{:S(2)}, u32[]{:S(2)}) collective-permute-start(bf16[1,8,8,128]{3,2,1,0:T(8,128)(2,1)} %get-tuple-element.112), channel_id=1, source_target_pairs={{16,0},{32,16},{48,32},{64,48},{80,64},{96,80},{112,96},{128,112},... | collective-permute-start | bytes 49160 | tf_op jit(solution)/shard_map/ppermute | solution.py:21
  17.6 19.6 %collective-permute-start.4 = (bf16[1,8,8,128]{3,2,1,0:T(8,128)(2,1)}, bf16[1,8,8,128]{3,2,1,0:T(8,128)(2,1)}, u32[]{:S(2)}, u32[]{:S(2)}) collective-permute-start(bf16[1,8,8,128]{3,2,1,0:T(8,128)(2,1)} %get-tuple-element.113), channel_id=1, source_target_pairs={{0,16},{16,32},{32,48},{48,64},{64,80},{80,96},{96,112},{112,128},... | collective-permute-start | bytes 49160 | tf_op jit(solution)/shard_map/ppermute | solution.py:19
  29.4 22.0 %collective-permute-start.2 = (bf16[6,1,4,256]{3,2,1,0:T(4,128)(2,1)}, bf16[6,1,4,256]{3,2,1,0:T(4,128)(2,1)S(1)}, u32[]{:S(2)}, u32[]{:S(2)}) collective-permute-start(bf16[6,1,4,256]{3,2,1,0:T(4,128)(2,1)} %get-tuple-element.155), channel_id=1, source_target_pairs={{0,1},{1,2},{2,3},{3,4},{4,5},{5,6},{6,7},{7,8},{8,9},{9,10},{10,1... | collective-permute-start | bytes 36872 | tf_op jit(solution)/shard_map/ppermute | solution.py:19
  35.3 16.1 %collective-permute-start.3 = (bf16[6,1,4,256]{3,2,1,0:T(4,128)(2,1)}, bf16[6,1,4,256]{3,2,1,0:T(4,128)(2,1)S(1)}, u32[]{:S(2)}, u32[]{:S(2)}) collective-permute-start(bf16[6,1,4,256]{3,2,1,0:T(4,128)(2,1)} %get-tuple-element.156), channel_id=1, source_target_pairs={{1,0},{2,1},{3,2},{4,3},{5,4},{6,5},{7,6},{8,7},{9,8},{10,9},{11,1... | collective-permute-start | bytes 36872 | tf_op jit(solution)/shard_map/ppermute | solution.py:21
  43.0 67.0 %collective-permute-start.6 = (bf16[10,1,8,128]{3,2,1,0:T(8,128)(2,1)}, bf16[10,1,8,128]{3,2,1,0:T(8,128)(2,1)}, u32[]{:S(2)}, u32[]{:S(2)}) collective-permute-start(bf16[10,1,8,128]{3,2,1,0:T(8,128)(2,1)} %get-tuple-element.67), channel_id=1, source_target_pairs={{0,1},{1,2},{2,3},{3,4},{4,5},{5,6},{6,7},{7,8},{8,9},{9,10},{10,1... | collective-permute-start | bytes 61448 | tf_op jit(solution)/shard_map/ppermute | solution.py:19
  48.1 61.8 %collective-permute-start.7 = (bf16[10,1,8,128]{3,2,1,0:T(8,128)(2,1)}, bf16[10,1,8,128]{3,2,1,0:T(8,128)(2,1)}, u32[]{:S(2)}, u32[]{:S(2)}) collective-permute-start(bf16[10,1,8,128]{3,2,1,0:T(8,128)(2,1)} %get-tuple-element.68), channel_id=1, source_target_pairs={{1,0},{2,1},{3,2},{4,3},{5,4},{6,5},{7,6},{8,7},{9,8},{10,9},{11,1... | collective-permute-start | bytes 61448 | tf_op jit(solution)/shard_map/ppermute | solution.py:21
  119.7 7.5 collective-permute-start.8
  128.4 8.3 %collective-permute-start.10 = (bf16[6,1,4,128]{3,2,1,0:T(4,128)(2,1)S(1)}, bf16[6,1,4,128]{3,2,1,0:T(4,128)(2,1)S(1)}, u32[]{:S(2)}, u32[]{:S(2)}) collective-permute-start(bf16[6,1,4,128]{3,2,1,0:T(4,128)(2,1)S(1)} %get-tuple-element.176), channel_id=1, source_target_pairs={{0,1},{1,2},{2,3},{3,4},{4,5},{5,6},{6,7},{7,8},{8,9},{9,10},{10,1... | collective-permute-start | bytes 18440 | tf_op jit(solution)/shard_map/ppermute | solution.py:19
  134.7 6.5 collective-permute-start.11
  149.8 15.7 %collective-permute-start.12 = (bf16[1,4,4,256]{3,2,1,0:T(4,128)(2,1)S(1)}, bf16[1,4,4,256]{3,2,1,0:T(4,128)(2,1)S(1)}, u32[]{:S(2)}, u32[]{:S(2)}) collective-permute-start(bf16[1,4,4,256]{3,2,1,0:T(4,128)(2,1)S(1)} %get-tuple-element.161), channel_id=1, source_target_pairs={{0,16},{16,32},{32,48},{48,64},{64,80},{80,96},{96,112},{112,128},... | collective-permute-start | bytes 24584 | tf_op jit(solution)/shard_map/ppermute | solution.py:19
  154.7 10.8 %collective-permute-start.13 = (bf16[1,4,4,256]{3,2,1,0:T(4,128)(2,1)S(1)}, bf16[1,4,4,256]{3,2,1,0:T(4,128)(2,1)S(1)}, u32[]{:S(2)}, u32[]{:S(2)}) collective-permute-start(bf16[1,4,4,256]{3,2,1,0:T(4,128)(2,1)S(1)} %get-tuple-element.162), channel_id=1, source_target_pairs={{16,0},{32,16},{48,32},{64,48},{80,64},{96,80},{112,96},{128,112},... | collective-permute-start | bytes 24584 | tf_op jit(solution)/shard_map/ppermute | solution.py:21
  166.1 8.5 %collective-permute-start.14 = (bf16[6,1,4,256]{3,2,1,0:T(4,128)(2,1)}, bf16[6,1,4,256]{3,2,1,0:T(4,128)(2,1)}, u32[]{:S(2)}, u32[]{:S(2)}) collective-permute-start(bf16[6,1,4,256]{3,2,1,0:T(4,128)(2,1)} %get-tuple-element.150), channel_id=1, source_target_pairs={{0,1},{1,2},{2,3},{3,4},{4,5},{5,6},{6,7},{7,8},{8,9},{9,10},{10,1... | collective-permute-start | bytes 36872 | tf_op jit(solution)/shard_map/ppermute | solution.py:19
  168.4 7.6 %collective-permute-start.15 = (bf16[6,1,4,256]{3,2,1,0:T(4,128)(2,1)}, bf16[6,1,4,256]{3,2,1,0:T(4,128)(2,1)}, u32[]{:S(2)}, u32[]{:S(2)}) collective-permute-start(bf16[6,1,4,256]{3,2,1,0:T(4,128)(2,1)} %get-tuple-element.151), channel_id=1, source_target_pairs={{1,0},{2,1},{3,2},{4,3},{5,4},{6,5},{7,6},{8,7},{9,8},{10,9},{11,1... | collective-permute-start | bytes 36872 | tf_op jit(solution)/shard_map/ppermute | solution.py:21
  266.1 147.4 %reduce-scatter.11.cloned.1.call-start = ((), (), s32[]{:S(2)}) async-start(), calls=%async_computation.8 | async-start | bytes 3760128 | tf_op jit(solution)/shard_map/reduce_scatter | solution.py:78
  280.3 227.7 %reduce-scatter.15.cloned.1.call-start = ((), (), s32[]{:S(2)}) async-start(), calls=%async_computation.10 | async-start | bytes 7520256 | tf_op jit(solution)/shard_map/reduce_scatter | solution.py:78
  289.6 6.7 collective-permute-start.22
  294.4 6.6 collective-permute-start.23
  326.8 257.8 %reduce-scatter.9.cloned.1.call-start = ((), (), s32[]{:S(2)}) async-start(), calls=%async_computation.7 | async-start | bytes 557056 | tf_op jit(solution)/shard_map/reduce_scatter | solution.py:79
  339.8 7.3 collective-permute-start.19
  355.2 307.6 %reduce-scatter.13.cloned.1.call-start = ((), (), s32[]{:S(2)}) async-start(), calls=%async_computation.9 | async-start | bytes 1114112 | tf_op jit(solution)/shard_map/reduce_scatter | solution.py:79
  415.8 328.7 %reduce-scatter.17.cloned.1.call-start = ((), (), s32[]{:S(2)}) async-start(), calls=%async_computation.11 | async-start | bytes 2228224 | tf_op jit(solution)/shard_map/reduce_scatter | solution.py:79
  (58 other events, 689.9 us)
Sparse Core Ops, SparseCore 0:
  266.2 68.0 reduce-scatter.6
  337.0 76.3 reduce-scatter.10
  416.2 91.7 reduce-scatter.14
  511.8 72.7 reduce-scatter.8
  589.1 73.6 reduce-scatter.12
  666.8 77.6 reduce-scatter.16
where the time goes:
time: 762 us; the launch traced here: 753 us
  waiting for transfers between devices  403 us (53%)
  matrix products  140 us (18%)
  local copies, waits for them, and re-layouts  104 us (14%)
  starting transfers between devices  73.8 us (10%)
  other arithmetic  16.3 us (2%)
  between operations  15.5 us (2%)
    reduce_scatter x3, waiting for transfers between devices, spread(): return lax.psum_scatter(partial_sum, 'gy', scatter_dimension=2, tiled=True)  229 us
    reduce_scatter x3, waiting for transfers between devices, spread(): partial_sum = lax.psum_scatter(term, 'gx', scatter_dimension=0, tiled=True)  150 us
    dot_general x81, matrix products, weight_grad(): lax.dot_general(piece, flat_grad, (((0,), (0,)), ((), ())), preferred_ele...  78.9 us
    reshape x53, local copies, waits for them, and re-layouts, adjoint(): ext[2 - i:2 - i + size_x, 2 - j:2 - j + size_y, 2 - k:2 - k + size_z]  73.3 us
    ppermute x12, starting transfers between devices, extended(): lax.ppermute(tail, axis, [(i, (i + 1) % count) for i in range(ends)])  53.2 us
    dot_general x81, matrix products, adjoint(): lax.dot_general(piece, weight[index], (((1,), (1,)), ((), ())), preferred...  50.5 us
    ppermute x12, waiting for transfers between devices, extended(): lax.ppermute(head, axis, [((i + 1) % count, i) for i in range(ends)])  24.3 us
    ppermute x12, starting transfers between devices, extended(): lax.ppermute(head, axis, [((i + 1) % count, i) for i in range(ends)])  20.4 us
  transfers between devices with their start and end apart: 30, of which 12 were waited for; matrix products, arithmetic and copies ran while one was open for 20% of the time, Pallas kernels for 0%

commit v1 on v0

v1 whole, which is shorter than its diff:
```python
import math

import jax
import jax.numpy as jnp
from jax import lax
from jax.experimental import pallas as pl
from jax.experimental.pallas import tpu as pltpu
from jax.sharding import PartitionSpec as P

MESH = pl.DeviceIdType.MESH
F32 = jnp.float32
BF16 = jnp.bfloat16

N = 16
BASE = 8
FX, FZ, C3 = 8, 8, 128
CX, CZ, C4 = 4, 4, 256
FR, CR = FX * FZ, CX * CZ
HALF = 14 * C3

FEAT, COT, POOL, DC, DF = range(5)
COT_T, POOL_G, ACT_G, DC_T, FINE, X_MID, X_DOWN, X_FINE = range(8)


def dot(a, b):
    return jnp.dot(a, b, preferred_element_type=F32)


def dot_t(a, b):
    return lax.dot_general(a, b, (((1,), (1,)), ((), ())), preferred_element_type=F32)


def own_rows(nz):
    return BASE + nz, BASE + nz + nz * (FX if nz == FZ else CX)


def put_own(ext, own, nz):
    lo, hi = own_rows(nz)
    nx = own.shape[0]
    ext[...] = jnp.zeros(ext.shape, F32)
    ext[1 : nx + 1, lo:hi, :] = own


def pack(ext, send_y, send_c, tmp, nz):
    lo, hi = own_rows(nz)
    nx = ext.shape[0] - 2
    chans = ext.shape[2]
    for side, start in ((0, lo), (1, hi - nz)):
        if nz == 8:
            send_y[side] = ext[1 : nx + 1, start : start + nz, :].reshape(nx * nz, chans).astype(BF16)
        else:
            for x in range(nx):
                tmp[side, nz * x : nz * x + nz, 0:chans] = ext[1 + x, start : start + nz, :]
            send_y[side] = tmp[side, 0 : nx * nz, 0:chans].astype(BF16)
        for end, x in ((0, 1), (1, nx)):
            send_c[2 * end + side] = ext[x, start : start + 16, :].astype(BF16)


def put_halo(ext, recv_x, recv_y, recv_c, inside, nz):
    lo, hi = own_rows(nz)
    nx = ext.shape[0] - 2
    chans = ext.shape[2]

    def kept(flag, value):
        return jnp.where(flag, value.astype(F32), 0.0)

    for end, x in ((0, 0), (1, nx + 1)):
        ext[x, lo:hi, :] = kept(inside[0][end], recv_x[end])
    for side, start in ((0, lo - nz), (1, hi)):
        line = kept(inside[1][side], recv_y[side])
        if nz == 8:
            ext[1 : nx + 1, start : start + nz, :] = line.reshape(nx, nz, chans)
        else:
            for x in range(nx):
                ext[1 + x, start : start + nz, :] = line[nz * x : nz * x + nz]
        for end, x in ((0, 0), (1, nx + 1)):
            flag = jnp.logical_and(inside[0][end], inside[1][side])
            ext[x, start : start + nz, :] = kept(flag, recv_c[2 * end + side])[0:nz]


def spread_lanes(ext, cols, nz):
    lo, hi = own_rows(nz)
    rows = hi - lo
    chans = ext.shape[2]
    z = lax.broadcasted_iota(jnp.int32, (rows, chans), 0) % nz

    def layer(x, carry):
        for b in range(3):
            for c in range(3):
                piece = ext[x, pl.ds(lo + nz * (b - 1) + c - 1, rows), :]
                if c == 0:
                    piece = jnp.where(z >= 1, piece, 0.0)
                if c == 2:
                    piece = jnp.where(z <= nz - 2, piece, 0.0)
                k = 3 * b + c
                cols[x, :, k * chans : (k + 1) * chans] = piece.astype(BF16)
        return carry

    lax.fori_loop(0, ext.shape[0], layer, 0)


def forward(cols, weight, nx):
    rows, depth = cols.shape[1], cols.shape[2]
    total = None
    for a in range(3):
        term = dot(
            cols[a : a + nx].reshape(nx * rows, depth),
            weight[9 * a : 9 * a + 9].reshape(depth, weight.shape[2]),
        )
        total = term if total is None else total + term
    return total


def backward(cols, weight, nx, total):
    rows = cols.shape[1]
    chans = weight.shape[2]
    for a in range(3):
        for k in range(9):
            piece = cols[a : a + nx, :, k * chans : (k + 1) * chans].reshape(nx * rows, chans)
            term = dot_t(piece, weight[26 - 9 * a - k])
            if a == 0 and k == 0:
                total[...] = term
            else:
                total[...] += term


def send_chunks(ext, flip, send_t):
    lo, hi = own_rows(CZ)
    flip[0:96, :] = ext[:, lo:hi, :].reshape(96, C4)
    flip[96:128, :] = jnp.zeros((32, C4), F32)
    send_t[...] = flip[...].T.astype(BF16)


def gather_lanes(recv_t, lines, shifted):
    lane = lax.broadcasted_iota(jnp.int32, (16, 128), 1) // 16
    for t in range(2):
        pieces = [recv_t[8 * t + s].astype(F32) for s in range(8)]
        for x in range(6):
            tile = jnp.zeros((16, 128), F32)
            for s in range(8):
                moved = pltpu.roll(pieces[s], (16 * s - 16 * x) % 128, 1) if s != x else pieces[s]
                tile = jnp.where(lane == s, moved, tile)
            lines[:, 256 * x + 128 * t : 256 * x + 128 * t + 128] = tile
    width = 6 * 256
    place = lax.broadcasted_iota(jnp.int32, (16, width), 1)
    z = place % CZ
    y = (place % 256) // CZ
    whole = lines[...]
    for b in range(3):
        for c in range(3):
            step = CZ * (b - 1) + c - 1
            moved = pltpu.roll(whole, (-step) % width, 1) if step else whole
            keep = (z + (c - 1) >= 0) & (z + (c - 1) < CZ) & (y + (b - 1) >= 0) & (y + (b - 1) < 64)
            k = 3 * b + c
            shifted[16 * k : 16 * k + 16, :] = jnp.where(keep, moved, 0.0).astype(BF16)


def coarse_grad(shifted, field, out):
    chans = field.shape[2]
    cells = field[...].reshape(1024, chans)
    out[432:512, 0:chans] = jnp.zeros((80, chans), F32)
    for a in range(3):
        term = dot(shifted[:, 256 * a : 256 * a + 1024], cells)
        for k in range(9):
            o = 26 - 9 * a - k
            out[16 * o : 16 * o + 16, 0:chans] = term[16 * k : 16 * k + 16]


def kernel(
    feat, cot, w_fine_hbm, w_down_hbm, w_mid_hbm,
    out_feat, out_fine, out_down, out_mid,
    w_fine, w_down, w_mid,
    ext_f, ext_c, ext_p, ext_d, ext_g,
    cols_f, cols_c, cols_p, cols_d, cols_g,
    own_p, own_d, own_g,
    sy_f, sc_f, rx_f, ry_f, rc_f,
    sy_c, sc_c, rx_c, ry_c, rc_c,
    sy_p, sc_p, rx_p, ry_p, rc_p,
    sy_d, sc_d, rx_d, ry_d, rc_d,
    sy_g, sc_g, rx_g, ry_g, rc_g,
    tmp, pairs, slope_f, delta_act, delta_pool, total_f,
    flip, lines, shifted_c, shifted_d, wide,
    st_c, rt_c, st_d, rt_d, all_p, all_a,
    part, send_f, recv_f, fold_f,
    sx_m, rx_m, sx_d, rx_d2, sx_f, rx_f2,
    w_sem, h_send, h_recv, a_send, a_recv,
):
    mx, my = lax.axis_index("gx"), lax.axis_index("gy")

    def other(axis, step):
        if axis == 0:
            return (lax.rem(mx + step, N), my)
        return (mx, lax.rem(my + step, N))

    loads = [
        pltpu.make_async_copy(src, dst, w_sem.at[i])
        for i, (src, dst) in enumerate(((w_fine_hbm, w_fine), (w_mid_hbm, w_mid), (w_down_hbm, w_down)))
    ]
    for load in loads:
        load.start()

    inside = ((mx > 0, mx < N - 1), (my > 0, my < N - 1))

    def neighbours(kind, first, last, send_y, send_c, recv_x, recv_y, recv_c):
        copies = []

        def add(src, dst, dx, dy):
            slot = len(copies)
            copies.append(
                pltpu.make_async_remote_copy(
                    src_ref=src,
                    dst_ref=dst,
                    send_sem=h_send.at[kind, slot],
                    recv_sem=h_recv.at[kind, slot],
                    device_id=(lax.rem(mx + dx + N, N), lax.rem(my + dy + N, N)),
                    device_id_type=MESH,
                )
            )

        add(first, recv_x.at[1], -1, 0)
        add(last, recv_x.at[0], 1, 0)
        for side in range(2):
            add(send_y.at[side], recv_y.at[1 - side], 0, 2 * side - 1)
        for end in range(2):
            for side in range(2):
                i = 2 * end + side
                add(send_c.at[i], recv_c.at[3 - i], 2 * end - 1, 2 * side - 1)
        return copies

    def exchange(kind, axis, src, dst):
        me = (mx, my)[axis]

        def copy(d, slot):
            return pltpu.make_async_remote_copy(
                src_ref=src(lax.rem(me + d, N)),
                dst_ref=dst(slot),
                send_sem=a_send.at[kind, d],
                recv_sem=a_recv.at[kind, d],
                device_id=other(axis, d),
                device_id_type=MESH,
            )

        def start():
            def body(d, carry):
                copy(d, me).start()
                return carry

            lax.fori_loop(1, N, body, 0)

        def arrive():
            def body(d, carry):
                copy(d, lax.rem(me - d + N, N)).wait_recv()
                return carry

            lax.fori_loop(1, N, body, 0)

        def leave():
            def body(d, carry):
                copy(d, me).wait_send()
                return carry

            lax.fori_loop(1, N, body, 0)

        return start, arrive, leave

    def sixteen(i):
        return pl.ds(pl.multiple_of(16 * i, 16), 16)

    halo_f = neighbours(FEAT, feat.at[0], feat.at[FX - 1], sy_f, sc_f, rx_f, ry_f, rc_f)
    halo_c = neighbours(COT, cot.at[0], cot.at[CX - 1], sy_c, sc_c, rx_c, ry_c, rc_c)
    halo_p = neighbours(POOL, own_p.at[0], own_p.at[CX - 1], sy_p, sc_p, rx_p, ry_p, rc_p)
    halo_d = neighbours(DC, own_d.at[0], own_d.at[CX - 1], sy_d, sc_d, rx_d, ry_d, rc_d)
    halo_g = neighbours(DF, own_g.at[0], own_g.at[FX - 1], sy_g, sc_g, rx_g, ry_g, rc_g)
    move_ct = exchange(COT_T, 1, lambda t: st_c.at[sixteen(t)], lambda s: rt_c.at[s])
    move_dt = exchange(DC_T, 1, lambda t: st_d.at[sixteen(t)], lambda s: rt_d.at[s])
    move_p = exchange(POOL_G, 1, lambda t: all_p.at[:, sixteen(my)], lambda s: all_p.at[:, sixteen(s)])
    move_a = exchange(ACT_G, 1, lambda t: all_a.at[:, sixteen(my)], lambda s: all_a.at[:, sixteen(s)])
    move_f = exchange(FINE, 1, lambda t: send_f.at[t], lambda s: recv_f.at[s])
    move_xm = exchange(X_MID, 0, lambda t: sx_m.at[t], lambda s: rx_m.at[s])
    move_xd = exchange(X_DOWN, 0, lambda t: sx_d.at[t], lambda s: rx_d2.at[s])
    move_xf = exchange(X_FINE, 0, lambda t: sx_f.at[t], lambda s: rx_f2.at[s])

    put_own(ext_f, feat[...].astype(F32), FZ)
    pack(ext_f, sy_f, sc_f, tmp, FZ)
    put_own(ext_c, cot[...].astype(F32), CZ)
    pack(ext_c, sy_c, sc_c, tmp, CZ)

    barrier = pltpu.get_barrier_semaphore()

    def greet(d, carry):
        for axis in range(2):
            pl.semaphore_signal(barrier, inc=1, device_id=other(axis, d), device_id_type=MESH)
        return carry

    lax.fori_loop(1, N, greet, 0)
    for dx in (1, N - 1):
        for dy in (1, N - 1):
            there = (lax.rem(mx + dx, N), lax.rem(my + dy, N))
            pl.semaphore_signal(barrier, inc=1, device_id=there, device_id_type=MESH)
    pl.semaphore_wait(barrier, 2 * (N - 1) + 4)

    for copy in halo_f + halo_c:
        copy.start()

    for copy in halo_f:
        copy.wait_recv()
    put_halo(ext_f, rx_f, ry_f, rc_f, inside, FZ)
    spread_lanes(ext_f, cols_f, FZ)
    loads[0].wait()
    pre = forward(cols_f, w_fine, FX)
    sig = jax.nn.sigmoid(pre)
    slope_f[...] = sig * (1.0 + pre * (1.0 - sig))
    act = (pre * sig).reshape(CX, 2, CX, 2, FZ, C3)
    pairs[...] = (act[:, 0, :, 0] + act[:, 0, :, 1] + act[:, 1, :, 0] + act[:, 1, :, 1]).reshape(128, C3)
    pooled = (pairs[pl.ds(0, 64, stride=2), :] + pairs[pl.ds(1, 64, stride=2), :]) * 0.125
    pooled = pooled.astype(BF16).reshape(CX, CR, C3)
    own_p[...] = pooled
    put_own(ext_p, pooled.astype(F32), CZ)
    pack(ext_p, sy_p, sc_p, tmp, CZ)
    for copy in halo_p:
        copy.start()
    all_p[:, sixteen(my), :] = pooled
    move_p[0]()

    for copy in halo_c:
        copy.wait_recv()
    put_halo(ext_c, rx_c, ry_c, rc_c, inside, CZ)
    send_chunks(ext_c, flip, st_c)
    move_ct[0]()
    rt_c[my] = st_c[sixteen(my), :]
    spread_lanes(ext_c, cols_c, CZ)
    loads[1].wait()
    backward(cols_c, w_mid, CX, delta_act)

    for copy in halo_p:
        copy.wait_recv()
    put_halo(ext_p, rx_p, ry_p, rc_p, inside, CZ)
    spread_lanes(ext_p, cols_p, CZ)
    loads[2].wait()
    pre = forward(cols_p, w_down, CX)
    sig = jax.nn.sigmoid(pre)
    delta = (delta_act[...] * (sig * (1.0 + pre * (1.0 - sig)))).astype(BF16).reshape(CX, CR, C4)
    own_d[...] = delta
    put_own(ext_d, delta.astype(F32), CZ)
    pack(ext_d, sy_d, sc_d, tmp, CZ)
    for copy in halo_d:
        copy.start()
    all_a[:, sixteen(my), :] = (pre * sig).astype(BF16).reshape(CX, CR, C4)
    move_a[0]()
    move_ct[1]()
    gather_lanes(rt_c, lines, shifted_c)

    for copy in halo_d:
        copy.wait_recv()
    put_halo(ext_d, rx_d, ry_d, rc_d, inside, CZ)
    spread_lanes(ext_d, cols_d, CZ)
    backward(cols_d, w_down, CX, delta_pool)
    pooled_delta = delta_pool[...] * 0.125
    pairs[pl.ds(0, 64, stride=2), :] = pooled_delta
    pairs[pl.ds(1, 64, stride=2), :] = pooled_delta
    up = jnp.broadcast_to(pairs[...].reshape(CX, 1, CX, 1, FZ, C3), (CX, 2, CX, 2, FZ, C3))
    delta = (up.reshape(512, C3) * slope_f[...]).astype(BF16)
    own_g[...] = delta.reshape(FX, FR, C3)
    put_own(ext_g, delta.astype(F32).reshape(FX, FR, C3), FZ)
    pack(ext_g, sy_g, sc_g, tmp, FZ)
    for copy in halo_g:
        copy.start()

    turned = ext_g[1 : FX + 1, BASE + FZ : BASE + FZ + FR, :].reshape(512, C3).T.astype(BF16)
    for a in range(3):
        part[:, 1152 * a : 1152 * a + 1152] = dot(turned, cols_f[a : a + FX].reshape(512, 1152))
    part[:, 27 * C3 : 28 * C3] = jnp.zeros((C3, C3), F32)

    def fold(j, carry):
        rows = pl.ds(pl.multiple_of(8 * j, 8), 8)
        send_f[j] = jnp.concatenate([part[rows, 0:HALF], part[rows, HALF : 2 * HALF]], axis=0).astype(BF16)
        return carry

    lax.fori_loop(0, N, fold, 0)
    move_f[0]()
    recv_f[my] = send_f[my]

    send_chunks(ext_d, flip, st_d)
    move_dt[0]()
    rt_d[my] = st_d[sixteen(my), :]

    move_a[1]()
    coarse_grad(shifted_c, all_a, wide)
    sx_m[...] = wide[...].T.astype(BF16).reshape(N, 16, 512)
    move_xm[0]()
    rx_m[mx] = sx_m[mx]

    for copy in halo_g:
        copy.wait_recv()
    put_halo(ext_g, rx_g, ry_g, rc_g, inside, FZ)
    spread_lanes(ext_g, cols_g, FZ)
    backward(cols_g, w_fine, FX, total_f)
    out_feat[...] = total_f[...].astype(BF16).reshape(FX, FR, C3)

    move_dt[1]()
    gather_lanes(rt_d, lines, shifted_d)
    move_p[1]()
    coarse_grad(shifted_d, all_p, wide)
    turned = wide[:, 0:C3].T
    for i in range(N):
        rows = turned[8 * i : 8 * i + 8]
        sx_d[i] = jnp.concatenate([rows[:, 0:256], rows[:, 256:512]], axis=0).astype(BF16)
    move_xd[0]()
    rx_d2[mx] = sx_d[mx]

    move_f[1]()

    def add_f(s, total):
        return total + recv_f[s].astype(F32)

    total = lax.fori_loop(0, N, add_f, jnp.zeros((16, HALF), F32))
    for o in range(28):
        half, at = divmod(o, 14)
        fold_f[8 * o : 8 * o + 8, :] = total[8 * half : 8 * half + 8, C3 * at : C3 * at + C3]
    fold_f[224:256, :] = jnp.zeros((32, C3), F32)
    turned = fold_f[...].T
    for i in range(N):
        rows = turned[8 * i : 8 * i + 8]
        sx_f[i] = jnp.concatenate([rows[:, 0:128], rows[:, 128:256]], axis=0).astype(BF16)
    move_xf[0]()
    rx_f2[mx] = sx_f[mx]

    def summed(arrived):
        def add(s, total):
            return total + arrived[s].astype(F32)

        return lax.fori_loop(0, N, add, jnp.zeros(arrived.shape[1:], F32))

    move_xm[1]()
    out_mid[...] = summed(rx_m) * (1.0 / math.sqrt(CX * N * CX * N * CZ))
    move_xd[1]()
    total = summed(rx_d2) * (1.0 / math.sqrt(CX * N * CX * N * CZ))
    out_down[:, 0:256] = total[0:8]
    out_down[:, 256:512] = total[8:16]
    move_xf[1]()
    total = summed(rx_f2) * (1.0 / math.sqrt(FX * N * FX * N * FZ))
    out_fine[:, 0:128] = total[0:8]
    out_fine[:, 128:256] = total[8:16]

    for copy in halo_f + halo_c + halo_p + halo_d + halo_g:
        copy.wait_send()
    for move in (move_ct, move_dt, move_p, move_a, move_f, move_xm, move_xd, move_xf):
        move[2]()


def halo_scratch(nx, rows, chans):
    lines = nx * rows // nx
    return [
        pltpu.VMEM((2, lines, chans), BF16),
        pltpu.VMEM((4, 16, chans), BF16),
        pltpu.VMEM((2, rows, chans), BF16),
        pltpu.VMEM((2, lines, chans), BF16),
        pltpu.VMEM((4, 16, chans), BF16),
    ]


def per_device(features, weight_fine, weight_down, weight_mid, cotangent):
    vmem = pl.BlockSpec(memory_space=pltpu.VMEM)
    anywhere = pl.BlockSpec(memory_space=pl.ANY)
    fine_ext = pltpu.VMEM((FX + 2, 2 * BASE + FZ * (FX + 2), C3), F32)
    fine_cols = pltpu.VMEM((FX + 2, FR, 9 * C3), BF16)

    def coarse_ext(chans):
        return pltpu.VMEM((CX + 2, 2 * BASE + CZ * (CX + 2), chans), F32)

    def coarse_cols(chans):
        return pltpu.VMEM((CX + 2, CR, 9 * chans), BF16)

    scratch = [
        pltpu.VMEM((27, C3, C3), BF16),
        pltpu.VMEM((27, C3, C4), BF16),
        pltpu.VMEM((27, C4, C4), BF16),
        fine_ext, coarse_ext(C4), coarse_ext(C3), coarse_ext(C4), fine_ext,
        fine_cols, coarse_cols(C4), coarse_cols(C3), coarse_cols(C4), fine_cols,
        pltpu.VMEM((CX, CR, C3), BF16),
        pltpu.VMEM((CX, CR, C4), BF16),
        pltpu.VMEM((FX, FR, C3), BF16),
        *halo_scratch(FX, FR, C3),
        *halo_scratch(CX, CR, C4),
        *halo_scratch(CX, CR, C3),
        *halo_scratch(CX, CR, C4),
        *halo_scratch(FX, FR, C3),
        pltpu.VMEM((2, 16, C4), F32),
        pltpu.VMEM((128, C3), F32),
        pltpu.VMEM((512, C3), F32),
        pltpu.VMEM((64, C4), F32),
        pltpu.VMEM((64, C3), F32),
        pltpu.VMEM((512, C3), F32),
        pltpu.VMEM((128, C4), F32),
        pltpu.VMEM((16, 6 * 256), F32),
        pltpu.VMEM((144, 6 * 256), BF16),
        pltpu.VMEM((144, 6 * 256), BF16),
        pltpu.VMEM((512, C4), F32),
        pltpu.VMEM((C4, 128), BF16),
        pltpu.VMEM((N, 16, 128), BF16),
        pltpu.VMEM((C4, 128), BF16),
        pltpu.VMEM((N, 16, 128), BF16),
        pltpu.VMEM((CX, N * CR, C3), BF16),
        pltpu.VMEM((CX, N * CR, C4), BF16),
        pltpu.VMEM((C3, 2 * HALF), F32),
        pltpu.VMEM((N, 16, HALF), BF16),
        pltpu.VMEM((N, 16, HALF), BF16),
        pltpu.VMEM((256, C3), F32),
        pltpu.VMEM((N, 16, 512), BF16),
        pltpu.VMEM((N, 16, 512), BF16),
        pltpu.VMEM((N, 16, 256), BF16),
        pltpu.VMEM((N, 16, 256), BF16),
        pltpu.VMEM((N, 16, 128), BF16),
        pltpu.VMEM((N, 16, 128), BF16),
        pltpu.SemaphoreType.DMA((3,)),
        pltpu.SemaphoreType.DMA((5, 8)),
        pltpu.SemaphoreType.DMA((5, 8)),
        pltpu.SemaphoreType.DMA((8, N)),
        pltpu.SemaphoreType.DMA((8, N)),
    ]
    out_feat, out_fine, out_down, out_mid = pl.pallas_call(
        kernel,
        out_shape=(
            jax.ShapeDtypeStruct((FX, FR, C3), BF16),
            jax.ShapeDtypeStruct((8, 256), F32),
            jax.ShapeDtypeStruct((8, 512), F32),
            jax.ShapeDtypeStruct((16, 512), F32),
        ),
        in_specs=[vmem, vmem, anywhere, anywhere, anywhere],
        out_specs=(vmem, vmem, vmem, vmem),
        scratch_shapes=scratch,
        compiler_params=pltpu.CompilerParams(
            collective_id=0, has_side_effects=True, vmem_limit_bytes=48 * 1024 * 1024
        ),
        name="unet_backward",
    )(
        features.reshape(FX, FR, C3),
        cotangent.reshape(CX, CR, C4),
        weight_fine,
        weight_down,
        weight_mid,
    )
    return (
        out_feat.reshape(FX, FX, FZ, C3),
        out_fine[:, : 27 * 8].reshape(8, 27, 8),
        out_down[:, : 27 * 16].reshape(8, 27, 16),
        out_mid[:, : 27 * 16].reshape(16, 27, 16),
    )


def solution(mesh):
    in_specs = (P("gx", "gy", None, None), P(), P(), P(), P("gx", "gy", None, None))
    out_specs = (
        P("gx", "gy", None, None),
        P("gx", None, "gy"),
        P("gx", None, "gy"),
        P("gx", None, "gy"),
    )
    return jax.shard_map(
        per_device, mesh=mesh, in_specs=in_specs, out_specs=out_specs, check_vma=False
    )
```

time: 762 us -> 67.2 us (0.09); the launches traced: 753 us -> 67 us
  waiting for transfers between devices: 403 us -> 0 us
  matrix products: 140 us -> 0 us
  local copies, waits for them, and re-layouts: 104 us -> 7.58 us
  starting transfers between devices: 73.8 us -> 0 us
  Pallas kernels: 0 us -> 58.7 us
  other arithmetic: 16.3 us -> 0 us
  between operations: 15.5 us -> 0.67 us
    reduce_scatter x6 -> x0, waiting for transfers between devices: 379 us -> none  [the longest x3 229 us: spread(): return lax.psum_scatter(partial_sum, 'gy', scatter_dimension=2, tiled=True)]
    dot_general x216 -> x0, matrix products: 140 us -> none  [the longest x81 78.9 us: weight_grad(): lax.dot_general(piece, flat_grad, (((0,), (0,)), ((), ())), preferred_ele...]
    reshape x55 -> x4, local copies, waits for them, and re-layouts: 76.3 us -> 1.09 us  [the longest x1 0.77 us: per_device(): cotangent.reshape(CX, CR, C4)]
    ppermute x24 -> x0, starting transfers between devices: 73.6 us -> none  [the longest x12 53.2 us: extended(): lax.ppermute(tail, axis, [(i, (i + 1) % count) for i in range(ends)])]
    pallas_call x0 -> x1, Pallas kernels: none -> 58.7 us  [per_device(): pl.pallas_call(kernel, out_shape=(jax.ShapeDtypeStruct((FX, FR, C3), BF16...]
    ppermute x24 -> x0, waiting for transfers between devices: 24.3 us -> none  [the longest x12 24.3 us: extended(): lax.ppermute(head, axis, [((i + 1) % count, i) for i in range(ends)])]
    slice x20 -> x0, local copies, waits for them, and re-layouts: 11.9 us -> none  [the longest x7 5.25 us: adjoint(): ext[2 - i:2 - i + size_x, 2 - j:2 - j + size_y, 2 - k:2 - k + size_z]]
    concatenate x14 -> x0, other arithmetic: 11 us -> none  [extended(): jnp.concatenate([lax.ppermute(tail, axis, [(i, (i + 1) % count) for i in...]
  transfers between devices with their start and end apart: 30 -> 0, of which waited for: 12 -> 0; matrix products, arithmetic and copies ran while one was open for 20% -> 0% of each run, Pallas kernels for 0% -> 0%
where the time goes in v1:
time: 67.2 us; the launch traced here: 67 us
  Pallas kernels  58.7 us (87%)
  local copies, waits for them, and re-layouts  7.58 us (11%)
    pallas_call x1, Pallas kernels, per_device(): pl.pallas_call(kernel, out_shape=(jax.ShapeDtypeStruct((FX, FR, C3), BF16...  58.7 us
    unnamed x10, local copies, waits for them, and re-layouts  6.49 us

profile of v1, /device:TPU:1, one launch (start us, length us, event | category | flops | bytes accessed | tf_op | source)
XLA Modules:
  0.0 67.0 jit_solution(16028342936314245451)
XLA Ops:
  0.6 0.8 %reshape.27.cot = bf16[4,16,256]{2,1,0:T(8,128)(2,1)S(1)} reshape(bf16[4,4,4,256]{3,2,1,0:T(4,128)(2,1)} %param.9) | data formatting | bytes 65536 | tf_op jit(solution)/shard_map/reshape | solution.py:538
  1.4 0.0 copy-start
  1.4 1.5 %copy-done = bf16[27,128,256]{2,1,0:T(8,128)(2,1)S(1)} copy-done((bf16[27,128,256]{2,1,0:T(8,128)(2,1)S(1)}, bf16[27,128,256]{2,1,0:T(8,128)(2,1)}, u32[]{:S(2)}) %copy-start) | copy-done | bytes 1769496
  2.9 0.0 copy-start.1
  2.9 1.2 %copy-done.1 = bf16[27,128,128]{2,1,0:T(8,128)(2,1)S(1)} copy-done((bf16[27,128,128]{2,1,0:T(8,128)(2,1)S(1)}, bf16[27,128,128]{2,1,0:T(8,128)(2,1)}, u32[]{:S(2)}) %copy-start.1) | copy-done | bytes 884760
  4.1 0.0 copy-start.2
  4.1 0.9 %copy-done.2 = bf16[8,8,8,128]{3,2,1,0:T(8,128)(2,1)S(1)} copy-done((bf16[8,8,8,128]{3,2,1,0:T(8,128)(2,1)S(1)}, bf16[8,8,8,128]{3,2,1,0:T(8,128)(2,1)}, u32[]{:S(2)}) %copy-start.2) | copy-done | bytes 131096
  5.0 58.7 %unet_backward.1 = (bf16[8,64,128]{2,1,0:T(8,128)(2,1)S(1)}, f32[8,256]{1,0:T(8,128)S(1)}, f32[8,512]{1,0:T(8,128)S(1)}, f32[16,512]{1,0:T(8,128)S(1)}) custom-call(bf16[8,64,128]{2,1,0:T(8,128)(2,1)S(1)} %bitcast.5, bf16[4,16,256]{2,1,0:T(8,128)(2,1)S(1)} %reshape.27.cot, bf16[27,128,128]{2,1,0:T(8,128)(2,1)S(1)} %copy-done.1, ...), custom_call_target="tpu_custom_call" | custom-call | tf_op jit(solution)/shard_map/unet_backward/pallas_call | solution.py:521
  63.7 0.1 reshape.31
  63.8 0.8 %copy.14 = f32[16,27,16]{1,2,0:T(8,128)} copy(f32[16,27,16]{2,1,0:T(8,128)S(1)} %reshape.31) | data formatting | bytes 55296
  64.6 0.1 reshape.30
  64.7 0.7 %copy.13 = f32[8,27,16]{1,2,0:T(8,128)} copy(f32[8,27,16]{2,1,0:T(8,128)S(1)} %reshape.30) | data formatting | bytes 27648
  65.5 0.1 reshape.29
  65.6 0.7 %copy.12 = f32[8,27,8]{1,2,0:T(8,128)} copy(f32[8,27,8]{2,1,0:T(8,128)S(1)} %reshape.29) | data formatting | bytes 13824
  66.3 0.7 copy.16
Async XLA Ops:
  1.4 1.5 %copy-start = (bf16[27,128,256]{2,1,0:T(8,128)(2,1)S(1)}, bf16[27,128,256]{2,1,0:T(8,128)(2,1)}, u32[]{:S(2)}) copy-start(bf16[27,128,256]{2,1,0:T(8,128)(2,1)} %w_down_hbm.1) | copy-start | bytes 5308420
  2.9 1.2 %copy-start.1 = (bf16[27,128,128]{2,1,0:T(8,128)(2,1)S(1)}, bf16[27,128,128]{2,1,0:T(8,128)(2,1)}, u32[]{:S(2)}) copy-start(bf16[27,128,128]{2,1,0:T(8,128)(2,1)} %w_fine_hbm.1) | copy-start | bytes 2654212
  4.1 0.9 %copy-start.2 = (bf16[8,8,8,128]{3,2,1,0:T(8,128)(2,1)S(1)}, bf16[8,8,8,128]{3,2,1,0:T(8,128)(2,1)}, u32[]{:S(2)}) copy-start(bf16[8,8,8,128]{3,2,1,0:T(8,128)(2,1)} %param.5) | copy-start | bytes 393220

commit v2 on v1

--- a/solution.py
+++ b/solution.py
@@ -16,7 +16,7 @@
 FX, FZ, C3 = 8, 8, 128
 CX, CZ, C4 = 4, 4, 256
 FR, CR = FX * FZ, CX * CZ
-HALF = 14 * C3
+HALF = 7 * C3
 
 FEAT, COT, POOL, DC, DF = range(5)
 COT_T, POOL_G, ACT_G, DC_T, FINE, X_MID, X_DOWN, X_FINE = range(8)
@@ -37,7 +37,6 @@
 def put_own(ext, own, nz):
     lo, hi = own_rows(nz)
     nx = own.shape[0]
-    ext[...] = jnp.zeros(ext.shape, F32)
     ext[1 : nx + 1, lo:hi, :] = own
 
 
@@ -127,7 +126,6 @@
 def send_chunks(ext, flip, send_t):
     lo, hi = own_rows(CZ)
     flip[0:96, :] = ext[:, lo:hi, :].reshape(96, C4)
-    flip[96:128, :] = jnp.zeros((32, C4), F32)
     send_t[...] = flip[...].T.astype(BF16)
 
 
@@ -158,18 +156,20 @@
 def coarse_grad(shifted, field, out):
     chans = field.shape[2]
     cells = field[...].reshape(1024, chans)
-    out[432:512, 0:chans] = jnp.zeros((80, chans), F32)
     for a in range(3):
         term = dot(shifted[:, 256 * a : 256 * a + 1024], cells)
         for k in range(9):
             o = 26 - 9 * a - k
-            out[16 * o : 16 * o + 16, 0:chans] = term[16 * k : 16 * k + 16]
+            for h in range(chans // 128):
+                out[h, pl.ds(o, 16, stride=32), :] = term[16 * k : 16 * k + 16, 128 * h : 128 * h + 128]
 
 
 def kernel(
-    feat, cot, w_fine_hbm, w_down_hbm, w_mid_hbm,
+    feat_hbm, cot_hbm, w_fine_hbm, w_down_hbm, w_mid_hbm,
     out_feat, out_fine, out_down, out_mid,
+    feat, cot, own_c,
     w_fine, w_down, w_mid,
+    ext_s, cols_s, border, border_s, turned_own, turned_s,
     ext_f, ext_c, ext_p, ext_d, ext_g,
     cols_f, cols_c, cols_p, cols_d, cols_g,
     own_p, own_d, own_g,
@@ -179,11 +179,11 @@
     sy_d, sc_d, rx_d, ry_d, rc_d,
     sy_g, sc_g, rx_g, ry_g, rc_g,
     tmp, pairs, slope_f, delta_act, delta_pool, total_f,
-    flip, lines, shifted_c, shifted_d, wide,
+    flip, lines, shifted_c, shifted_d, wide, spread,
     st_c, rt_c, st_d, rt_d, all_p, all_a,
     part, send_f, recv_f, fold_f,
     sx_m, rx_m, sx_d, rx_d2, sx_f, rx_f2,
-    w_sem, h_send, h_recv, a_send, a_recv,
+    w_sem, s_send, s_recv, h_send, h_recv, a_send, a_recv,
 ):
     mx, my = lax.axis_index("gx"), lax.axis_index("gy")
 
@@ -192,9 +192,30 @@
             return (lax.rem(mx + step, N), my)
         return (mx, lax.rem(my + step, N))
 
+    barrier = pltpu.get_barrier_semaphore()
+
+    def greet(d, carry):
+        for axis in range(2):
+            pl.semaphore_signal(barrier, inc=1, device_id=other(axis, d), device_id_type=MESH)
+        return carry
+
+    lax.fori_loop(1, N, greet, 0)
+    for dx in (1, N - 1):
+        for dy in (1, N - 1):
+            there = (lax.rem(mx + dx, N), lax.rem(my + dy, N))
+            pl.semaphore_signal(barrier, inc=1, device_id=there, device_id_type=MESH)
+
     loads = [
         pltpu.make_async_copy(src, dst, w_sem.at[i])
-        for i, (src, dst) in enumerate(((w_fine_hbm, w_fine), (w_mid_hbm, w_mid), (w_down_hbm, w_down)))
+        for i, (src, dst) in enumerate(
+            (
+                (feat_hbm, feat),
+                (cot_hbm, cot),
+                (w_fine_hbm, w_fine),
+                (w_mid_hbm, w_mid),
+                (w_down_hbm, w_down),
+            )
+        )
     ]
     for load in loads:
         load.start()
@@ -267,7 +288,7 @@
         return pl.ds(pl.multiple_of(16 * i, 16), 16)
 
     halo_f = neighbours(FEAT, feat.at[0], feat.at[FX - 1], sy_f, sc_f, rx_f, ry_f, rc_f)
-    halo_c = neighbours(COT, cot.at[0], cot.at[CX - 1], sy_c, sc_c, rx_c, ry_c, rc_c)
+    halo_c = neighbours(COT, own_c.at[0], own_c.at[CX - 1], sy_c, sc_c, rx_c, ry_c, rc_c)
     halo_p = neighbours(POOL, own_p.at[0], own_p.at[CX - 1], sy_p, sc_p, rx_p, ry_p, rc_p)
     halo_d = neighbours(DC, own_d.at[0], own_d.at[CX - 1], sy_d, sc_d, rx_d, ry_d, rc_d)
     halo_g = neighbours(DF, own_g.at[0], own_g.at[FX - 1], sy_g, sc_g, rx_g, ry_g, rc_g)
@@ -280,33 +301,43 @@
     move_xd = exchange(X_DOWN, 0, lambda t: sx_d.at[t], lambda s: rx_d2.at[s])
     move_xf = exchange(X_FINE, 0, lambda t: sx_f.at[t], lambda s: rx_f2.at[s])
 
+    core = lax.rem(my, 2)
+    sibling = (mx, my + 1 - 2 * core)
+
+    def to_sibling(i, src, dst):
+        return pltpu.make_async_remote_copy(
+            src_ref=src,
+            dst_ref=dst,
+            send_sem=s_send.at[i],
+            recv_sem=s_recv.at[i],
+            device_id=sibling,
+            device_id_type=MESH,
+        )
+
+    sib_feat = to_sibling(0, border, border_s)
+    sib_delta = to_sibling(1, turned_own, turned_s)
+
+    loads[0].wait()
     put_own(ext_f, feat[...].astype(F32), FZ)
     pack(ext_f, sy_f, sc_f, tmp, FZ)
-    put_own(ext_c, cot[...].astype(F32), CZ)
+    pl.semaphore_wait(barrier, 2 * (N - 1) + 4)
+    for copy in halo_f:
+        copy.start()
+    loads[1].wait()
+    lo, hi = own_rows(CZ)
+    for x in range(CX):
+        for y in range(CX):
+            ext_c[1 + x, lo + CZ * y : lo + CZ * y + CZ, :] = cot[x, y].astype(F32)
+    own_c[...] = ext_c[1 : CX + 1, lo:hi, :].astype(BF16)
     pack(ext_c, sy_c, sc_c, tmp, CZ)
-
-    barrier = pltpu.get_barrier_semaphore()
-
-    def greet(d, carry):
-        for axis in range(2):
-            pl.semaphore_signal(barrier, inc=1, device_id=other(axis, d), device_id_type=MESH)
-        return carry
-
-    lax.fori_loop(1, N, greet, 0)
-    for dx in (1, N - 1):
-        for dy in (1, N - 1):
-            there = (lax.rem(mx + dx, N), lax.rem(my + dy, N))
-            pl.semaphore_signal(barrier, inc=1, device_id=there, device_id_type=MESH)
-    pl.semaphore_wait(barrier, 2 * (N - 1) + 4)
-
-    for copy in halo_f + halo_c:
+    for copy in halo_c:
         copy.start()
 
     for copy in halo_f:
         copy.wait_recv()
     put_halo(ext_f, rx_f, ry_f, rc_f, inside, FZ)
     spread_lanes(ext_f, cols_f, FZ)
-    loads[0].wait()
+    loads[2].wait()
     pre = forward(cols_f, w_fine, FX)
     sig = jax.nn.sigmoid(pre)
     slope_f[...] = sig * (1.0 + pre * (1.0 - sig))
@@ -319,6 +350,8 @@
     pack(ext_p, sy_p, sc_p, tmp, CZ)
     for copy in halo_p:
         copy.start()
+    border[...] = ext_f[:, BASE : BASE + FZ * (FX + 2), :].astype(BF16)
+    sib_feat.start()
     all_p[:, sixteen(my), :] = pooled
     move_p[0]()
 
@@ -329,14 +362,14 @@
     move_ct[0]()
     rt_c[my] = st_c[sixteen(my), :]
     spread_lanes(ext_c, cols_c, CZ)
-    loads[1].wait()
+    loads[3].wait()
     backward(cols_c, w_mid, CX, delta_act)
 
     for copy in halo_p:
         copy.wait_recv()
     put_halo(ext_p, rx_p, ry_p, rc_p, inside, CZ)
     spread_lanes(ext_p, cols_p, CZ)
-    loads[2].wait()
+    loads[4].wait()
     pre = forward(cols_p, w_down, CX)
     sig = jax.nn.sigmoid(pre)
     delta = (delta_act[...] * (sig * (1.0 + pre * (1.0 - sig)))).astype(BF16).reshape(CX, CR, C4)
@@ -347,6 +380,9 @@
         copy.start()
     all_a[:, sixteen(my), :] = (pre * sig).astype(BF16).reshape(CX, CR, C4)
     move_a[0]()
+    sib_feat.wait_recv()
+    ext_s[:, BASE : BASE + FZ * (FX + 2), :] = border_s[...].astype(F32)
+    spread_lanes(ext_s, cols_s, FZ)
     move_ct[1]()
     gather_lanes(rt_c, lines, shifted_c)
 
@@ -360,35 +396,54 @@
     pairs[pl.ds(1, 64, stride=2), :] = pooled_delta
     up = jnp.broadcast_to(pairs[...].reshape(CX, 1, CX, 1, FZ, C3), (CX, 2, CX, 2, FZ, C3))
     delta = (up.reshape(512, C3) * slope_f[...]).astype(BF16)
+    turned_own[...] = delta.astype(F32).T.astype(BF16)
+    sib_delta.start()
+    send_chunks(ext_d, flip, st_d)
+    move_dt[0]()
+    rt_d[my] = st_d[sixteen(my), :]
+
+    lanes = pl.ds(pl.multiple_of(4 * C3 * core, C3), 5 * C3)
+
+    def half(turned, cols):
+        part[:, 0 : 9 * C3] += dot(turned, cols[pl.ds(2 * core, FX)].reshape(512, 9 * C3))
+        part[:, 9 * C3 : 14 * C3] += dot(turned, cols[1 : 1 + FX, :, lanes].reshape(512, 5 * C3))
+
+    part[...] = jnp.zeros(part.shape, F32)
+    half(turned_own[...], cols_f)
+    sib_delta.wait_recv()
+    half(turned_s[...], cols_s)
+
+    def fold(j, carry):
+        rows = pl.ds(pl.multiple_of(8 * j, 8), 8)
+        send_f[j] = jnp.concatenate([part[rows, 0:HALF], part[rows, HALF : 2 * HALF]], axis=0).astype(BF16)
+        return carry
+
+    lax.fori_loop(0, N, fold, 0)
+    move_f[0]()
+    recv_f[my] = send_f[my]
     own_g[...] = delta.reshape(FX, FR, C3)
     put_own(ext_g, delta.astype(F32).reshape(FX, FR, C3), FZ)
     pack(ext_g, sy_g, sc_g, tmp, FZ)
     for copy in halo_g:
         copy.start()
 
-    turned = ext_g[1 : FX + 1, BASE + FZ : BASE + FZ + FR, :].reshape(512, C3).T.astype(BF16)
-    for a in range(3):
-        part[:, 1152 * a : 1152 * a + 1152] = dot(turned, cols_f[a : a + FX].reshape(512, 1152))
-    part[:, 27 * C3 : 28 * C3] = jnp.zeros((C3, C3), F32)
-
-    def fold(j, carry):
-        rows = pl.ds(pl.multiple_of(8 * j, 8), 8)
-        send_f[j] = jnp.concatenate([part[rows, 0:HALF], part[rows, HALF : 2 * HALF]], axis=0).astype(BF16)
-        return carry
-
-    lax.fori_loop(0, N, fold, 0)
-    move_f[0]()
-    recv_f[my] = send_f[my]
-
-    send_chunks(ext_d, flip, st_d)
-    move_dt[0]()
-    rt_d[my] = st_d[sixteen(my), :]
-
     move_a[1]()
     coarse_grad(shifted_c, all_a, wide)
-    sx_m[...] = wide[...].T.astype(BF16).reshape(N, 16, 512)
+    for h in range(2):
+        sx_m[8 * h : 8 * h + 8] = wide[h].T.astype(BF16).reshape(8, 16, 512)
     move_xm[0]()
     rx_m[mx] = sx_m[mx]
+
+    move_dt[1]()
+    gather_lanes(rt_d, lines, shifted_d)
+    move_p[1]()
+    coarse_grad(shifted_d, all_p, wide)
+    turned = wide[0].T
+    for i in range(N):
+        rows = turned[8 * i : 8 * i + 8]
+        sx_d[i] = jnp.concatenate([rows[:, 0:256], rows[:, 256:512]], axis=0).astype(BF16)
+    move_xd[0]()
+    rx_d2[mx] = sx_d[mx]
 
     for copy in halo_g:
         copy.wait_recv()
@@ -397,27 +452,17 @@
     backward(cols_g, w_fine, FX, total_f)
     out_feat[...] = total_f[...].astype(BF16).reshape(FX, FR, C3)
 
-    move_dt[1]()
-    gather_lanes(rt_d, lines, shifted_d)
-    move_p[1]()
-    coarse_grad(shifted_d, all_p, wide)
-    turned = wide[:, 0:C3].T
-    for i in range(N):
-        rows = turned[8 * i : 8 * i + 8]
-        sx_d[i] = jnp.concatenate([rows[:, 0:256], rows[:, 256:512]], axis=0).astype(BF16)
-    move_xd[0]()
-    rx_d2[mx] = sx_d[mx]
-
     move_f[1]()
 
-    def add_f(s, total):
-        return total + recv_f[s].astype(F32)
-
-    total = lax.fori_loop(0, N, add_f, jnp.zeros((16, HALF), F32))
-    for o in range(28):
-        half, at = divmod(o, 14)
-        fold_f[8 * o : 8 * o + 8, :] = total[8 * half : 8 * half + 8, C3 * at : C3 * at + C3]
-    fold_f[224:256, :] = jnp.zeros((32, C3), F32)
+    def add_f(s, totals):
+        return tuple(totals[c] + recv_f[2 * s + c].astype(F32) for c in range(2))
+
+    nothing = jnp.zeros((16, HALF), F32)
+    totals = lax.fori_loop(0, N // 2, add_f, (nothing, nothing))
+    for o in range(27):
+        c, i = (0, o) if o < 14 else (1, o - 18 if o >= 18 else o - 4)
+        half_at, at = divmod(i, 7)
+        fold_f[pl.ds(o, 8, stride=32), :] = totals[c][8 * half_at : 8 * half_at + 8, C3 * at : C3 * at + C3]
     turned = fold_f[...].T
     for i in range(N):
         rows = turned[8 * i : 8 * i + 8]
@@ -431,18 +476,25 @@
 
         return lax.fori_loop(0, N, add, jnp.zeros(arrived.shape[1:], F32))
 
+    def unfold(out, total, rows, first, most):
+        for co in range(first, first + most):
+            at = 32 * (co - first)
+            spread[pl.ds(co, rows, stride=out.shape[0] // rows), 0:32] = total[:, at : at + 32]
+        out[...] = spread[0 : out.shape[0], 0:27]
+
+    coarse_scale = 1.0 / math.sqrt(CX * N * CX * N * CZ)
     move_xm[1]()
-    out_mid[...] = summed(rx_m) * (1.0 / math.sqrt(CX * N * CX * N * CZ))
+    unfold(out_mid, summed(rx_m) * coarse_scale, 16, 0, 16)
     move_xd[1]()
-    total = summed(rx_d2) * (1.0 / math.sqrt(CX * N * CX * N * CZ))
-    out_down[:, 0:256] = total[0:8]
-    out_down[:, 256:512] = total[8:16]
+    total = summed(rx_d2) * coarse_scale
+    unfold(out_down, total[0:8], 8, 0, 8)
+    unfold(out_down, total[8:16], 8, 8, 8)
     move_xf[1]()
     total = summed(rx_f2) * (1.0 / math.sqrt(FX * N * FX * N * FZ))
-    out_fine[:, 0:128] = total[0:8]
-    out_fine[:, 128:256] = total[8:16]
-
-    for copy in halo_f + halo_c + halo_p + halo_d + halo_g:
+    unfold(out_fine, total[0:8], 8, 0, 4)
+    unfold(out_fine, total[8:16], 8, 4, 4)
+
+    for copy in halo_f + halo_c + halo_p + halo_d + halo_g + [sib_feat, sib_delta]:
         copy.wait_send()
     for move in (move_ct, move_dt, move_p, move_a, move_f, move_xm, move_xd, move_xf):
         move[2]()
@@ -459,9 +511,14 @@
     ]
 
 
+def hand_over(*refs):
+    for i in range(4):
+        refs[4 + i][...] = refs[i][...]
+
+
 def per_device(features, weight_fine, weight_down, weight_mid, cotangent):
     vmem = pl.BlockSpec(memory_space=pltpu.VMEM)
-    anywhere = pl.BlockSpec(memory_space=pl.ANY)
+    hbm = pl.BlockSpec(memory_space=pltpu.HBM)
     fine_ext = pltpu.VMEM((FX + 2, 2 * BASE + FZ * (FX + 2), C3), F32)
     fine_cols = pltpu.VMEM((FX + 2, FR, 9 * C3), BF16)
 
@@ -472,9 +529,17 @@
         return pltpu.VMEM((CX + 2, CR, 9 * chans), BF16)
 
     scratch = [
+        pltpu.VMEM((FX, FR, C3), BF16),
+        pltpu.VMEM((CX, CX, CZ, C4), BF16),
+        pltpu.VMEM((CX, CR, C4), BF16),
         pltpu.VMEM((27, C3, C3), BF16),
         pltpu.VMEM((27, C3, C4), BF16),
         pltpu.VMEM((27, C4, C4), BF16),
+        fine_ext, fine_cols,
+        pltpu.VMEM((FX + 2, FZ * (FX + 2), C3), BF16),
+        pltpu.VMEM((FX + 2, FZ * (FX + 2), C3), BF16),
+        pltpu.VMEM((C3, 512), BF16),
+        pltpu.VMEM((C3, 512), BF16),
         fine_ext, coarse_ext(C4), coarse_ext(C3), coarse_ext(C4), fine_ext,
         fine_cols, coarse_cols(C4), coarse_cols(C3), coarse_cols(C4), fine_cols,
         pltpu.VMEM((CX, CR, C3), BF16),
@@ -495,7 +560,8 @@
         pltpu.VMEM((16, 6 * 256), F32),
         pltpu.VMEM((144, 6 * 256), BF16),
         pltpu.VMEM((144, 6 * 256), BF16),
-        pltpu.VMEM((512, C4), F32),
+        pltpu.VMEM((2, 512, 128), F32),
+        pltpu.VMEM((16 * 16, 128), F32),
         pltpu.VMEM((C4, 128), BF16),
         pltpu.VMEM((N, 16, 128), BF16),
         pltpu.VMEM((C4, 128), BF16),
@@ -512,39 +578,49 @@
         pltpu.VMEM((N, 16, 256), BF16),
         pltpu.VMEM((N, 16, 128), BF16),
         pltpu.VMEM((N, 16, 128), BF16),
-        pltpu.SemaphoreType.DMA((3,)),
+        pltpu.SemaphoreType.DMA((5,)),
+        pltpu.SemaphoreType.DMA((2,)),
+        pltpu.SemaphoreType.DMA((2,)),
         pltpu.SemaphoreType.DMA((5, 8)),
         pltpu.SemaphoreType.DMA((5, 8)),
         pltpu.SemaphoreType.DMA((8, N)),
         pltpu.SemaphoreType.DMA((8, N)),
     ]
-    out_feat, out_fine, out_down, out_mid = pl.pallas_call(
+    shapes = (
+            jax.ShapeDtypeStruct((FX, FR, C3), BF16),
+            jax.ShapeDtypeStruct((8 * 8, 27), F32),
+            jax.ShapeDtypeStruct((8 * 16, 27), F32),
+            jax.ShapeDtypeStruct((16 * 16, 27), F32),
+    )
+    results = pl.pallas_call(
         kernel,
-        out_shape=(
-            jax.ShapeDtypeStruct((FX, FR, C3), BF16),
-            jax.ShapeDtypeStruct((8, 256), F32),
-            jax.ShapeDtypeStruct((8, 512), F32),
-            jax.ShapeDtypeStruct((16, 512), F32),
-        ),
-        in_specs=[vmem, vmem, anywhere, anywhere, anywhere],
+        out_shape=shapes,
+        in_specs=[hbm] * 5,
         out_specs=(vmem, vmem, vmem, vmem),
         scratch_shapes=scratch,
         compiler_params=pltpu.CompilerParams(
-            collective_id=0, has_side_effects=True, vmem_limit_bytes=48 * 1024 * 1024
+            collective_id=0, has_side_effects=True, vmem_limit_bytes=61 * 1024 * 1024
         ),
         name="unet_backward",
     )(
         features.reshape(FX, FR, C3),
-        cotangent.reshape(CX, CR, C4),
+        cotangent,
         weight_fine,
         weight_down,
         weight_mid,
     )
+    out_feat, out_fine, out_down, out_mid = pl.pallas_call(
+        hand_over,
+        out_shape=shapes,
+        in_specs=[vmem] * 4,
+        out_specs=(vmem,) * 4,
+        name="hand_over",
+    )(*results)
     return (
         out_feat.reshape(FX, FX, FZ, C3),
-        out_fine[:, : 27 * 8].reshape(8, 27, 8),
-        out_down[:, : 27 * 16].reshape(8, 27, 16),
-        out_mid[:, : 27 * 16].reshape(16, 27, 16),
+        out_fine.reshape(8, 8, 27).transpose(0, 2, 1),
+        out_down.reshape(8, 16, 27).transpose(0, 2, 1),
+        out_mid.reshape(16, 16, 27).transpose(0, 2, 1),
     )
 
 

time: 67.2 us -> 57.6 us (0.86)
  the two profiles are of different devices: /device:TPU:1 before, /device:TPU:2 now
where the time goes in v2:
time: 57.6 us; the launch traced here: 57.5 us
  Pallas kernels  56.8 us (99%)
  between operations  0.64 us (1%)
    pallas_call x1, Pallas kernels, per_device(): pl.pallas_call(kernel, out_shape=shapes, in_specs=[hbm] * 5, out_specs=(v...  55.1 us
    pallas_call x1, Pallas kernels, per_device(): pl.pallas_call(hand_over, out_shape=shapes, in_specs=[vmem] * 4, out_spec...  1.76 us

profile of v2, /device:TPU:2, one launch (start us, length us, event | category | flops | bytes accessed | tf_op | source)
XLA Modules:
  0.0 57.5 jit_solution(8577756849087174531)
XLA Ops:
  0.6 55.1 %unet_backward.1 = (bf16[8,64,128]{2,1,0:T(8,128)(2,1)}, f32[64,27]{1,0:T(8,128)}, f32[128,27]{1,0:T(8,128)}, f32[256,27]{1,0:T(8,128)}) custom-call(bf16[8,64,128]{2,1,0:T(8,128)(2,1)} %bitcast.11, bf16[4,4,4,256]{3,2,1,0:T(4,128)(2,1)} %cot_hbm.1, bf16[27,128,128]{2,1,0:T(8,128)(2,1)} %w_fine_hbm.1, bf16[27,128,256]{2,1,0:T(8,128)(2,1)} %w_down_hbm.1, ...), custom_call_target="tpu_custom_call" | custom-call | tf_op jit(solution)/shard_map/unet_backward/pallas_call | solution.py:595
  55.7 1.8 %hand_over.1 = (bf16[8,64,128]{2,1,0:T(8,128)(2,1)}, f32[64,27]{1,0:T(8,128)}, f32[128,27]{1,0:T(8,128)}, f32[256,27]{1,0:T(8,128)}) custom-call(bf16[8,64,128]{2,1,0:T(8,128)(2,1)} %get-tuple-element.12.refs_0_, f32[64,27]{1,0:T(8,128)} %get-tuple-element.13.refs_1_, f32[128,27]{1,0:T(8,128)} %get-tuple-element.14.refs_2_, f32[256,27]{1,0:T(8,128)} %get-tuple-element.15.refs_3_), custom_call_target="tpu_custom_call" | custom-call | tf_op jit(solution)/shard_map/hand_over/pallas_call | solution.py:612

commit v3 on v2

--- a/solution.py
+++ b/solution.py
@@ -18,7 +18,7 @@
 FR, CR = FX * FZ, CX * CZ
 HALF = 7 * C3
 
-FEAT, COT, POOL, DC, DF = range(5)
+FEAT, COT, POOL, DF = range(4)
 COT_T, POOL_G, ACT_G, DC_T, FINE, X_MID, X_DOWN, X_FINE = range(8)
 
 
@@ -30,56 +30,50 @@
     return lax.dot_general(a, b, (((1,), (1,)), ((), ())), preferred_element_type=F32)
 
 
-def own_rows(nz):
-    return BASE + nz, BASE + nz + nz * (FX if nz == FZ else CX)
-
-
-def put_own(ext, own, nz):
-    lo, hi = own_rows(nz)
-    nx = own.shape[0]
-    ext[1 : nx + 1, lo:hi, :] = own
-
-
-def pack(ext, send_y, send_c, tmp, nz):
-    lo, hi = own_rows(nz)
-    nx = ext.shape[0] - 2
+def kept(flag, value):
+    return jnp.where(flag, value.astype(F32), 0.0)
+
+
+def frame(reach):
+    nx, nz = (FX, FZ) if reach == 1 else (CX, CZ)
+    lo = BASE + 8
+    return nx, lo, lo + nx * nz
+
+
+def put_own(ext, own, reach):
+    nx, lo, hi = frame(reach)
+    ext[reach : reach + nx, lo:hi, :] = own
+
+
+def pack(ext, send_y, send_c, reach):
+    nx, lo, hi = frame(reach)
     chans = ext.shape[2]
-    for side, start in ((0, lo), (1, hi - nz)):
-        if nz == 8:
-            send_y[side] = ext[1 : nx + 1, start : start + nz, :].reshape(nx * nz, chans).astype(BF16)
-        else:
-            for x in range(nx):
-                tmp[side, nz * x : nz * x + nz, 0:chans] = ext[1 + x, start : start + nz, :]
-            send_y[side] = tmp[side, 0 : nx * nz, 0:chans].astype(BF16)
-        for end, x in ((0, 1), (1, nx)):
-            send_c[2 * end + side] = ext[x, start : start + 16, :].astype(BF16)
-
-
-def put_halo(ext, recv_x, recv_y, recv_c, inside, nz):
-    lo, hi = own_rows(nz)
-    nx = ext.shape[0] - 2
+    for side, start in ((0, lo), (1, hi - 8)):
+        send_y[side] = ext[reach : reach + nx, start : start + 8, :].reshape(nx * 8, chans).astype(BF16)
+        for end, x in ((0, reach), (1, nx)):
+            if reach == 1:
+                send_c[2 * end + side] = ext[x, start : start + 16, :].astype(BF16)
+            else:
+                send_c[2 * end + side] = ext[x : x + 2, start : start + 8, :].reshape(16, chans).astype(BF16)
+
+
+def put_halo(ext, recv_x, recv_y, recv_c, inside, reach):
+    nx, lo, hi = frame(reach)
     chans = ext.shape[2]
-
-    def kept(flag, value):
-        return jnp.where(flag, value.astype(F32), 0.0)
-
-    for end, x in ((0, 0), (1, nx + 1)):
-        ext[x, lo:hi, :] = kept(inside[0][end], recv_x[end])
-    for side, start in ((0, lo - nz), (1, hi)):
+    for end, x in ((0, 0), (1, reach + nx)):
+        ext[x : x + reach, lo:hi, :] = kept(inside[0][end], recv_x[end]).reshape(reach, hi - lo, chans)
+    for side, start in ((0, lo - 8), (1, hi)):
         line = kept(inside[1][side], recv_y[side])
-        if nz == 8:
-            ext[1 : nx + 1, start : start + nz, :] = line.reshape(nx, nz, chans)
-        else:
-            for x in range(nx):
-                ext[1 + x, start : start + nz, :] = line[nz * x : nz * x + nz]
-        for end, x in ((0, 0), (1, nx + 1)):
+        ext[reach : reach + nx, start : start + 8, :] = line.reshape(nx, 8, chans)
+        for end, x in ((0, 0), (1, reach + nx)):
             flag = jnp.logical_and(inside[0][end], inside[1][side])
-            ext[x, start : start + nz, :] = kept(flag, recv_c[2 * end + side])[0:nz]
+            corner = kept(flag, recv_c[2 * end + side])[0 : 8 * reach]
+            ext[x : x + reach, start : start + 8, :] = corner.reshape(reach, 8, chans)
 
 
 def spread_lanes(ext, cols, nz):
-    lo, hi = own_rows(nz)
-    rows = hi - lo
+    lo = BASE + nz
+    rows = cols.shape[1]
     chans = ext.shape[2]
     z = lax.broadcasted_iota(jnp.int32, (rows, chans), 0) % nz
 
@@ -123,9 +117,8 @@
                 total[...] += term
 
 
-def send_chunks(ext, flip, send_t):
-    lo, hi = own_rows(CZ)
-    flip[0:96, :] = ext[:, lo:hi, :].reshape(96, C4)
+def send_chunks(layers, flip, send_t):
+    flip[0:96, :] = layers.reshape(96, C4)
     send_t[...] = flip[...].T.astype(BF16)
 
 
@@ -172,13 +165,12 @@
     ext_s, cols_s, border, border_s, turned_own, turned_s,
     ext_f, ext_c, ext_p, ext_d, ext_g,
     cols_f, cols_c, cols_p, cols_d, cols_g,
-    own_p, own_d, own_g,
+    own_p, own_g,
     sy_f, sc_f, rx_f, ry_f, rc_f,
     sy_c, sc_c, rx_c, ry_c, rc_c,
     sy_p, sc_p, rx_p, ry_p, rc_p,
-    sy_d, sc_d, rx_d, ry_d, rc_d,
     sy_g, sc_g, rx_g, ry_g, rc_g,
-    tmp, pairs, slope_f, delta_act, delta_pool, total_f,
+    act_c, pairs, slope_f, delta_act, delta_pool, total_f,
     flip, lines, shifted_c, shifted_d, wide, spread,
     st_c, rt_c, st_d, rt_d, all_p, all_a,
     part, send_f, recv_f, fold_f,
@@ -288,9 +280,8 @@
         return pl.ds(pl.multiple_of(16 * i, 16), 16)
 
     halo_f = neighbours(FEAT, feat.at[0], feat.at[FX - 1], sy_f, sc_f, rx_f, ry_f, rc_f)
-    halo_c = neighbours(COT, own_c.at[0], own_c.at[CX - 1], sy_c, sc_c, rx_c, ry_c, rc_c)
-    halo_p = neighbours(POOL, own_p.at[0], own_p.at[CX - 1], sy_p, sc_p, rx_p, ry_p, rc_p)
-    halo_d = neighbours(DC, own_d.at[0], own_d.at[CX - 1], sy_d, sc_d, rx_d, ry_d, rc_d)
+    halo_c = neighbours(COT, own_c.at[0:2], own_c.at[CX - 2 : CX], sy_c, sc_c, rx_c, ry_c, rc_c)
+    halo_p = neighbours(POOL, own_p.at[0:2], own_p.at[CX - 2 : CX], sy_p, sc_p, rx_p, ry_p, rc_p)
     halo_g = neighbours(DF, own_g.at[0], own_g.at[FX - 1], sy_g, sc_g, rx_g, ry_g, rc_g)
     move_ct = exchange(COT_T, 1, lambda t: st_c.at[sixteen(t)], lambda s: rt_c.at[s])
     move_dt = exchange(DC_T, 1, lambda t: st_d.at[sixteen(t)], lambda s: rt_d.at[s])
@@ -318,24 +309,24 @@
     sib_delta = to_sibling(1, turned_own, turned_s)
 
     loads[0].wait()
-    put_own(ext_f, feat[...].astype(F32), FZ)
-    pack(ext_f, sy_f, sc_f, tmp, FZ)
+    put_own(ext_f, feat[...].astype(F32), 1)
+    pack(ext_f, sy_f, sc_f, 1)
     pl.semaphore_wait(barrier, 2 * (N - 1) + 4)
     for copy in halo_f:
         copy.start()
     loads[1].wait()
-    lo, hi = own_rows(CZ)
+    nx, lo, hi = frame(2)
     for x in range(CX):
         for y in range(CX):
-            ext_c[1 + x, lo + CZ * y : lo + CZ * y + CZ, :] = cot[x, y].astype(F32)
-    own_c[...] = ext_c[1 : CX + 1, lo:hi, :].astype(BF16)
-    pack(ext_c, sy_c, sc_c, tmp, CZ)
+            ext_c[2 + x, lo + CZ * y : lo + CZ * y + CZ, :] = cot[x, y].astype(F32)
+    own_c[...] = ext_c[2 : CX + 2, lo:hi, :].astype(BF16)
+    pack(ext_c, sy_c, sc_c, 2)
     for copy in halo_c:
         copy.start()
 
     for copy in halo_f:
         copy.wait_recv()
-    put_halo(ext_f, rx_f, ry_f, rc_f, inside, FZ)
+    put_halo(ext_f, rx_f, ry_f, rc_f, inside, 1)
     spread_lanes(ext_f, cols_f, FZ)
     loads[2].wait()
     pre = forward(cols_f, w_fine, FX)
@@ -346,8 +337,8 @@
     pooled = (pairs[pl.ds(0, 64, stride=2), :] + pairs[pl.ds(1, 64, stride=2), :]) * 0.125
     pooled = pooled.astype(BF16).reshape(CX, CR, C3)
     own_p[...] = pooled
-    put_own(ext_p, pooled.astype(F32), CZ)
-    pack(ext_p, sy_p, sc_p, tmp, CZ)
+    put_own(ext_p, pooled.astype(F32), 2)
+    pack(ext_p, sy_p, sc_p, 2)
     for copy in halo_p:
         copy.start()
     border[...] = ext_f[:, BASE : BASE + FZ * (FX + 2), :].astype(BF16)
@@ -357,38 +348,35 @@
 
     for copy in halo_c:
         copy.wait_recv()
-    put_halo(ext_c, rx_c, ry_c, rc_c, inside, CZ)
-    send_chunks(ext_c, flip, st_c)
+    put_halo(ext_c, rx_c, ry_c, rc_c, inside, 2)
+    send_chunks(ext_c[1:7, lo:hi, :], flip, st_c)
     move_ct[0]()
     rt_c[my] = st_c[sixteen(my), :]
     spread_lanes(ext_c, cols_c, CZ)
     loads[3].wait()
-    backward(cols_c, w_mid, CX, delta_act)
-
-    for copy in halo_p:
-        copy.wait_recv()
-    put_halo(ext_p, rx_p, ry_p, rc_p, inside, CZ)
-    spread_lanes(ext_p, cols_p, CZ)
-    loads[4].wait()
-    pre = forward(cols_p, w_down, CX)
-    sig = jax.nn.sigmoid(pre)
-    delta = (delta_act[...] * (sig * (1.0 + pre * (1.0 - sig)))).astype(BF16).reshape(CX, CR, C4)
-    own_d[...] = delta
-    put_own(ext_d, delta.astype(F32), CZ)
-    pack(ext_d, sy_d, sc_d, tmp, CZ)
-    for copy in halo_d:
-        copy.start()
-    all_a[:, sixteen(my), :] = (pre * sig).astype(BF16).reshape(CX, CR, C4)
-    move_a[0]()
+    backward(cols_c, w_mid, CX + 2, delta_act)
     sib_feat.wait_recv()
     ext_s[:, BASE : BASE + FZ * (FX + 2), :] = border_s[...].astype(F32)
     spread_lanes(ext_s, cols_s, FZ)
-    move_ct[1]()
-    gather_lanes(rt_c, lines, shifted_c)
-
-    for copy in halo_d:
+
+    for copy in halo_p:
         copy.wait_recv()
-    put_halo(ext_d, rx_d, ry_d, rc_d, inside, CZ)
+    put_halo(ext_p, rx_p, ry_p, rc_p, inside, 2)
+    spread_lanes(ext_p, cols_p, CZ)
+    loads[4].wait()
+    pre = forward(cols_p, w_down, CX + 2)
+    sig = jax.nn.sigmoid(pre)
+    act_c[...] = (pre * sig).reshape(CX + 2, 32, C4)
+    all_a[:, sixteen(my), :] = act_c[1 : CX + 1, CZ : CZ + CR, :].astype(BF16)
+    move_a[0]()
+    delta = (delta_act[...] * (sig * (1.0 + pre * (1.0 - sig)))).astype(BF16).astype(F32)
+    last = BASE + CZ * (CX + 2)
+    ext_d[:, BASE:last, :] = delta.reshape(CX + 2, 32, C4)[:, 0 : CZ * (CX + 2), :]
+    for end, x in ((0, 0), (1, CX + 1)):
+        ext_d[x, BASE:last, :] = kept(inside[0][end], ext_d[x, BASE:last, :])
+    for side, start in ((0, BASE), (1, last - CZ)):
+        ext_d[:, start : start + CZ, :] = kept(inside[1][side], ext_d[:, start : start + CZ, :])
+
     spread_lanes(ext_d, cols_d, CZ)
     backward(cols_d, w_down, CX, delta_pool)
     pooled_delta = delta_pool[...] * 0.125
@@ -398,7 +386,7 @@
     delta = (up.reshape(512, C3) * slope_f[...]).astype(BF16)
     turned_own[...] = delta.astype(F32).T.astype(BF16)
     sib_delta.start()
-    send_chunks(ext_d, flip, st_d)
+    send_chunks(ext_d[:, 12:28, :], flip, st_d)
     move_dt[0]()
     rt_d[my] = st_d[sixteen(my), :]
 
@@ -410,6 +398,9 @@
 
     part[...] = jnp.zeros(part.shape, F32)
     half(turned_own[...], cols_f)
+    move_ct[1]()
+    gather_lanes(rt_c, lines, shifted_c)
+
     sib_delta.wait_recv()
     half(turned_s[...], cols_s)
 
@@ -422,8 +413,8 @@
     move_f[0]()
     recv_f[my] = send_f[my]
     own_g[...] = delta.reshape(FX, FR, C3)
-    put_own(ext_g, delta.astype(F32).reshape(FX, FR, C3), FZ)
-    pack(ext_g, sy_g, sc_g, tmp, FZ)
+    put_own(ext_g, delta.astype(F32).reshape(FX, FR, C3), 1)
+    pack(ext_g, sy_g, sc_g, 1)
     for copy in halo_g:
         copy.start()
 
@@ -444,13 +435,6 @@
         sx_d[i] = jnp.concatenate([rows[:, 0:256], rows[:, 256:512]], axis=0).astype(BF16)
     move_xd[0]()
     rx_d2[mx] = sx_d[mx]
-
-    for copy in halo_g:
-        copy.wait_recv()
-    put_halo(ext_g, rx_g, ry_g, rc_g, inside, FZ)
-    spread_lanes(ext_g, cols_g, FZ)
-    backward(cols_g, w_fine, FX, total_f)
-    out_feat[...] = total_f[...].astype(BF16).reshape(FX, FR, C3)
 
     move_f[1]()
 
@@ -470,6 +454,13 @@
     move_xf[0]()
     rx_f2[mx] = sx_f[mx]
 
+    for copy in halo_g:
+        copy.wait_recv()
+    put_halo(ext_g, rx_g, ry_g, rc_g, inside, 1)
+    spread_lanes(ext_g, cols_g, FZ)
+    backward(cols_g, w_fine, FX, total_f)
+    out_feat[...] = total_f[...].astype(BF16).reshape(FX, FR, C3)
+
     def summed(arrived):
         def add(s, total):
             return total + arrived[s].astype(F32)
@@ -494,18 +485,18 @@
     unfold(out_fine, total[0:8], 8, 0, 4)
     unfold(out_fine, total[8:16], 8, 4, 4)
 
-    for copy in halo_f + halo_c + halo_p + halo_d + halo_g + [sib_feat, sib_delta]:
+    for copy in halo_f + halo_c + halo_p + halo_g + [sib_feat, sib_delta]:
         copy.wait_send()
     for move in (move_ct, move_dt, move_p, move_a, move_f, move_xm, move_xd, move_xf):
         move[2]()
 
 
-def halo_scratch(nx, rows, chans):
-    lines = nx * rows // nx
+def halo_scratch(lines, layers):
+    chans = layers[-1]
     return [
         pltpu.VMEM((2, lines, chans), BF16),
         pltpu.VMEM((4, 16, chans), BF16),
-        pltpu.VMEM((2, rows, chans), BF16),
+        pltpu.VMEM((2, *layers), BF16),
         pltpu.VMEM((2, lines, chans), BF16),
         pltpu.VMEM((4, 16, chans), BF16),
     ]
@@ -522,11 +513,14 @@
     fine_ext = pltpu.VMEM((FX + 2, 2 * BASE + FZ * (FX + 2), C3), F32)
     fine_cols = pltpu.VMEM((FX + 2, FR, 9 * C3), BF16)
 
-    def coarse_ext(chans):
-        return pltpu.VMEM((CX + 2, 2 * BASE + CZ * (CX + 2), chans), F32)
-
-    def coarse_cols(chans):
-        return pltpu.VMEM((CX + 2, CR, 9 * chans), BF16)
+    def wide_ext(chans):
+        return pltpu.VMEM((CX + 4, 3 * BASE + CZ * (CX + 4), chans), F32)
+
+    def wide_cols(chans):
+        return pltpu.VMEM((CX + 4, 32, 9 * chans), BF16)
+
+    ext_d = pltpu.VMEM((CX + 2, 2 * BASE + CZ * (CX + 2), C4), F32)
+    cols_d = pltpu.VMEM((CX + 2, CR, 9 * C4), BF16)
 
     scratch = [
         pltpu.VMEM((FX, FR, C3), BF16),
@@ -540,20 +534,18 @@
         pltpu.VMEM((FX + 2, FZ * (FX + 2), C3), BF16),
         pltpu.VMEM((C3, 512), BF16),
         pltpu.VMEM((C3, 512), BF16),
-        fine_ext, coarse_ext(C4), coarse_ext(C3), coarse_ext(C4), fine_ext,
-        fine_cols, coarse_cols(C4), coarse_cols(C3), coarse_cols(C4), fine_cols,
+        fine_ext, wide_ext(C4), wide_ext(C3), ext_d, fine_ext,
+        fine_cols, wide_cols(C4), wide_cols(C3), cols_d, fine_cols,
         pltpu.VMEM((CX, CR, C3), BF16),
-        pltpu.VMEM((CX, CR, C4), BF16),
         pltpu.VMEM((FX, FR, C3), BF16),
-        *halo_scratch(FX, FR, C3),
-        *halo_scratch(CX, CR, C4),
-        *halo_scratch(CX, CR, C3),
-        *halo_scratch(CX, CR, C4),
-        *halo_scratch(FX, FR, C3),
-        pltpu.VMEM((2, 16, C4), F32),
+        *halo_scratch(FR, (FR, C3)),
+        *halo_scratch(32, (2, CR, C4)),
+        *halo_scratch(32, (2, CR, C3)),
+        *halo_scratch(FR, (FR, C3)),
+        pltpu.VMEM((CX + 2, 32, C4), F32),
         pltpu.VMEM((128, C3), F32),
         pltpu.VMEM((512, C3), F32),
-        pltpu.VMEM((64, C4), F32),
+        pltpu.VMEM((6 * 32, C4), F32),
         pltpu.VMEM((64, C3), F32),
         pltpu.VMEM((512, C3), F32),
         pltpu.VMEM((128, C4), F32),
@@ -581,8 +573,8 @@
         pltpu.SemaphoreType.DMA((5,)),
         pltpu.SemaphoreType.DMA((2,)),
         pltpu.SemaphoreType.DMA((2,)),
-        pltpu.SemaphoreType.DMA((5, 8)),
-        pltpu.SemaphoreType.DMA((5, 8)),
+        pltpu.SemaphoreType.DMA((4, 8)),
+        pltpu.SemaphoreType.DMA((4, 8)),
         pltpu.SemaphoreType.DMA((8, N)),
         pltpu.SemaphoreType.DMA((8, N)),
     ]

time: 57.6 us -> 52.7 us (0.915)
  the two profiles are of different devices: /device:TPU:2 before, /device:TPU:1 now
where the time goes in v3:
time: 52.7 us; the launch traced here: 52.6 us
  Pallas kernels  52 us (99%)
  between operations  0.64 us (1%)
    pallas_call x1, Pallas kernels, per_device(): pl.pallas_call(kernel, out_shape=shapes, in_specs=[hbm] * 5, out_specs=(v...  50.2 us
    pallas_call x1, Pallas kernels, per_device(): pl.pallas_call(hand_over, out_shape=shapes, in_specs=[vmem] * 4, out_spec...  1.76 us

profile of v3, /device:TPU:1, one launch (start us, length us, event | category | flops | bytes accessed | tf_op | source)
XLA Modules:
  0.0 52.6 jit_solution(2461130799785846452)
XLA Ops:
  0.6 50.2 %unet_backward.1 = (bf16[8,64,128]{2,1,0:T(8,128)(2,1)}, f32[64,27]{1,0:T(8,128)}, f32[128,27]{1,0:T(8,128)}, f32[256,27]{1,0:T(8,128)}) custom-call(bf16[8,64,128]{2,1,0:T(8,128)(2,1)} %bitcast.11, bf16[4,4,4,256]{3,2,1,0:T(4,128)(2,1)} %cot_hbm.1, bf16[27,128,128]{2,1,0:T(8,128)(2,1)} %w_fine_hbm.1, bf16[27,128,256]{2,1,0:T(8,128)(2,1)} %w_down_hbm.1, ...), custom_call_target="tpu_custom_call" | custom-call | tf_op jit(solution)/shard_map/unet_backward/pallas_call | solution.py:587
  50.9 1.8 %hand_over.1 = (bf16[8,64,128]{2,1,0:T(8,128)(2,1)}, f32[64,27]{1,0:T(8,128)}, f32[128,27]{1,0:T(8,128)}, f32[256,27]{1,0:T(8,128)}) custom-call(bf16[8,64,128]{2,1,0:T(8,128)(2,1)} %get-tuple-element.12.refs_0_, f32[64,27]{1,0:T(8,128)} %get-tuple-element.13.refs_1_, f32[128,27]{1,0:T(8,128)} %get-tuple-element.14.refs_2_, f32[256,27]{1,0:T(8,128)} %get-tuple-element.15.refs_3_), custom_call_target="tpu_custom_call" | custom-call | tf_op jit(solution)/shard_map/hand_over/pallas_call | solution.py:604

commit v4 on v3

--- a/solution.py
+++ b/solution.py
@@ -286,7 +286,6 @@
     move_ct = exchange(COT_T, 1, lambda t: st_c.at[sixteen(t)], lambda s: rt_c.at[s])
     move_dt = exchange(DC_T, 1, lambda t: st_d.at[sixteen(t)], lambda s: rt_d.at[s])
     move_p = exchange(POOL_G, 1, lambda t: all_p.at[:, sixteen(my)], lambda s: all_p.at[:, sixteen(s)])
-    move_a = exchange(ACT_G, 1, lambda t: all_a.at[:, sixteen(my)], lambda s: all_a.at[:, sixteen(s)])
     move_f = exchange(FINE, 1, lambda t: send_f.at[t], lambda s: recv_f.at[s])
     move_xm = exchange(X_MID, 0, lambda t: sx_m.at[t], lambda s: rx_m.at[s])
     move_xd = exchange(X_DOWN, 0, lambda t: sx_d.at[t], lambda s: rx_d2.at[s])
@@ -304,6 +303,49 @@
             device_id=sibling,
             device_id_type=MESH,
         )
+
+    def block_a(slot, i, device):
+        return pltpu.make_async_remote_copy(
+            src_ref=all_a.at[:, sixteen(slot)],
+            dst_ref=all_a.at[:, sixteen(slot)],
+            send_sem=a_send.at[ACT_G, i],
+            recv_sem=a_recv.at[ACT_G, i],
+            device_id=device,
+            device_id_type=MESH,
+        )
+
+    beside = sibling[1]
+
+    def seven(step):
+        def body(k, carry):
+            step(k, lax.rem(my + 2 * k, N), lax.rem(my - 2 * k + N, N), lax.rem(beside - 2 * k + N, N))
+            return carry
+
+        lax.fori_loop(1, N // 2, body, 0)
+
+    def start_a():
+        block_a(my, 1, sibling).start()
+        seven(lambda k, to, came, other_came: block_a(my, 2 * k, (mx, to)).start())
+
+    def forward_a():
+        def step(k, to, came, other_came):
+            block_a(came, 2 * k, (mx, to)).wait_recv()
+            block_a(came, 2 * k + 1, sibling).start()
+
+        seven(step)
+
+    def arrive_a():
+        block_a(beside, 1, sibling).wait_recv()
+        seven(lambda k, to, came, other_came: block_a(other_came, 2 * k + 1, sibling).wait_recv())
+
+    def leave_a():
+        block_a(my, 1, sibling).wait_send()
+
+        def step(k, to, came, other_came):
+            block_a(my, 2 * k, (mx, to)).wait_send()
+            block_a(came, 2 * k + 1, sibling).wait_send()
+
+        seven(step)
 
     sib_feat = to_sibling(0, border, border_s)
     sib_delta = to_sibling(1, turned_own, turned_s)
@@ -368,7 +410,7 @@
     sig = jax.nn.sigmoid(pre)
     act_c[...] = (pre * sig).reshape(CX + 2, 32, C4)
     all_a[:, sixteen(my), :] = act_c[1 : CX + 1, CZ : CZ + CR, :].astype(BF16)
-    move_a[0]()
+    start_a()
     delta = (delta_act[...] * (sig * (1.0 + pre * (1.0 - sig)))).astype(BF16).astype(F32)
     last = BASE + CZ * (CX + 2)
     ext_d[:, BASE:last, :] = delta.reshape(CX + 2, 32, C4)[:, 0 : CZ * (CX + 2), :]
@@ -412,13 +454,14 @@
     lax.fori_loop(0, N, fold, 0)
     move_f[0]()
     recv_f[my] = send_f[my]
+    forward_a()
     own_g[...] = delta.reshape(FX, FR, C3)
     put_own(ext_g, delta.astype(F32).reshape(FX, FR, C3), 1)
     pack(ext_g, sy_g, sc_g, 1)
     for copy in halo_g:
         copy.start()
 
-    move_a[1]()
+    arrive_a()
     coarse_grad(shifted_c, all_a, wide)
     for h in range(2):
         sx_m[8 * h : 8 * h + 8] = wide[h].T.astype(BF16).reshape(8, 16, 512)
@@ -487,7 +530,8 @@
 
     for copy in halo_f + halo_c + halo_p + halo_g + [sib_feat, sib_delta]:
         copy.wait_send()
-    for move in (move_ct, move_dt, move_p, move_a, move_f, move_xm, move_xd, move_xf):
+    leave_a()
+    for move in (move_ct, move_dt, move_p, move_f, move_xm, move_xd, move_xf):
         move[2]()
 
 

time: 52.7 us -> 50.2 us (0.953)
  Pallas kernels: 52 us -> 49.5 us
    pallas_call x1, Pallas kernels: 50.2 us -> 47.8 us  [per_device(): pl.pallas_call(kernel, out_shape=shapes, in_specs=[hbm] * 5, out_specs=(v...]
where the time goes in v4:
time: 50.2 us; the launch traced here: 50.1 us
  Pallas kernels  49.5 us (99%)
  between operations  0.64 us (1%)
    pallas_call x1, Pallas kernels, per_device(): pl.pallas_call(kernel, out_shape=shapes, in_specs=[hbm] * 5, out_specs=(v...  47.8 us
    pallas_call x1, Pallas kernels, per_device(): pl.pallas_call(hand_over, out_shape=shapes, in_specs=[vmem] * 4, out_spec...  1.76 us

profile of v4, /device:TPU:1, one launch (start us, length us, event | category | flops | bytes accessed | tf_op | source)
XLA Modules:
  0.0 50.1 jit_solution(231687525413253015)
XLA Ops:
  0.6 47.8 %unet_backward.1 = (bf16[8,64,128]{2,1,0:T(8,128)(2,1)}, f32[64,27]{1,0:T(8,128)}, f32[128,27]{1,0:T(8,128)}, f32[256,27]{1,0:T(8,128)}) custom-call(bf16[8,64,128]{2,1,0:T(8,128)(2,1)} %bitcast.11, bf16[4,4,4,256]{3,2,1,0:T(4,128)(2,1)} %cot_hbm.1, bf16[27,128,128]{2,1,0:T(8,128)(2,1)} %w_fine_hbm.1, bf16[27,128,256]{2,1,0:T(8,128)(2,1)} %w_down_hbm.1, ...), custom_call_target="tpu_custom_call" | custom-call | tf_op jit(solution)/shard_map/unet_backward/pallas_call | solution.py:631
  48.4 1.8 %hand_over.1 = (bf16[8,64,128]{2,1,0:T(8,128)(2,1)}, f32[64,27]{1,0:T(8,128)}, f32[128,27]{1,0:T(8,128)}, f32[256,27]{1,0:T(8,128)}) custom-call(bf16[8,64,128]{2,1,0:T(8,128)(2,1)} %get-tuple-element.12.refs_0_, f32[64,27]{1,0:T(8,128)} %get-tuple-element.13.refs_1_, f32[128,27]{1,0:T(8,128)} %get-tuple-element.14.refs_2_, f32[256,27]{1,0:T(8,128)} %get-tuple-element.15.refs_3_), custom_call_target="tpu_custom_call" | custom-call | tf_op jit(solution)/shard_map/hand_over/pallas_call | solution.py:648

commit v5 on v4

--- a/solution.py
+++ b/solution.py
@@ -461,13 +461,6 @@
     for copy in halo_g:
         copy.start()
 
-    arrive_a()
-    coarse_grad(shifted_c, all_a, wide)
-    for h in range(2):
-        sx_m[8 * h : 8 * h + 8] = wide[h].T.astype(BF16).reshape(8, 16, 512)
-    move_xm[0]()
-    rx_m[mx] = sx_m[mx]
-
     move_dt[1]()
     gather_lanes(rt_d, lines, shifted_d)
     move_p[1]()
@@ -478,6 +471,13 @@
         sx_d[i] = jnp.concatenate([rows[:, 0:256], rows[:, 256:512]], axis=0).astype(BF16)
     move_xd[0]()
     rx_d2[mx] = sx_d[mx]
+
+    arrive_a()
+    coarse_grad(shifted_c, all_a, wide)
+    for h in range(2):
+        sx_m[8 * h : 8 * h + 8] = wide[h].T.astype(BF16).reshape(8, 16, 512)
+    move_xm[0]()
+    rx_m[mx] = sx_m[mx]
 
     move_f[1]()
 

time: 50.2 us -> 50.5 us (level)
  no operation moved by 1% of the time
where the time goes in v5:
time: 50.5 us; the launch traced here: 50.4 us
  Pallas kernels  49.7 us (98%)
  between operations  0.64 us (1%)
    pallas_call x1, Pallas kernels, per_device(): pl.pallas_call(kernel, out_shape=shapes, in_specs=[hbm] * 5, out_specs=(v...  48 us
    pallas_call x1, Pallas kernels, per_device(): pl.pallas_call(hand_over, out_shape=shapes, in_specs=[vmem] * 4, out_spec...  1.76 us

profile of v5, /device:TPU:1, one launch (start us, length us, event | category | flops | bytes accessed | tf_op | source)
XLA Modules:
  0.0 50.4 jit_solution(13500050281641328927)
XLA Ops:
  0.6 48.0 %unet_backward.1 = (bf16[8,64,128]{2,1,0:T(8,128)(2,1)}, f32[64,27]{1,0:T(8,128)}, f32[128,27]{1,0:T(8,128)}, f32[256,27]{1,0:T(8,128)}) custom-call(bf16[8,64,128]{2,1,0:T(8,128)(2,1)} %bitcast.11, bf16[4,4,4,256]{3,2,1,0:T(4,128)(2,1)} %cot_hbm.1, bf16[27,128,128]{2,1,0:T(8,128)(2,1)} %w_fine_hbm.1, bf16[27,128,256]{2,1,0:T(8,128)(2,1)} %w_down_hbm.1, ...), custom_call_target="tpu_custom_call" | custom-call | tf_op jit(solution)/shard_map/unet_backward/pallas_call | solution.py:631
  48.6 1.8 %hand_over.1 = (bf16[8,64,128]{2,1,0:T(8,128)(2,1)}, f32[64,27]{1,0:T(8,128)}, f32[128,27]{1,0:T(8,128)}, f32[256,27]{1,0:T(8,128)}) custom-call(bf16[8,64,128]{2,1,0:T(8,128)(2,1)} %get-tuple-element.12.refs_0_, f32[64,27]{1,0:T(8,128)} %get-tuple-element.13.refs_1_, f32[128,27]{1,0:T(8,128)} %get-tuple-element.14.refs_2_, f32[256,27]{1,0:T(8,128)} %get-tuple-element.15.refs_3_), custom_call_target="tpu_custom_call" | custom-call | tf_op jit(solution)/shard_map/hand_over/pallas_call | solution.py:648
